TPU v7x, 256 devices: a whole 4x4x8 slice. The times are simulated.
256 devices in a mesh: section: 4 (over x), seq: 16 (over y, z_hi, core), mp: 4 (over z_lo).
Axes of the slice: x: 4, y: 4, z: 8 (z_hi: 2, z_lo: 4; z = z_hi * 4 + z_lo), core: 2. Of those that a mesh axis runs over, the one named last changes fastest.
Arguments:
- rows40: bfloat16 [3072, 8192], P('seq', ('section', 'mp')), may hold values from -6 to 6
- queries: bfloat16 [4, 3072, 4096], P('section', 'seq', 'mp'), may hold values from -200 to 200, as said below
- kv_weight: bfloat16 [4, 8192, 1024], P('section', 'seq', 'mp'), may hold values from -0.0625 to 0.0625
- out_grad: bfloat16 [4, 3072, 4096], P('section', 'seq', 'mp'), may hold values from -6 to 6
- block_order: int32 [64], replicated, may hold values from 0 to 63, each once
Outputs:
- attended: bfloat16 [4, 3072, 4096], P('section', 'seq', 'mp')
- query_grad: bfloat16 [4, 3072, 4096], P('section', 'seq', 'mp')
- kv_weight_grad: float32 [4, 8192, 1024], P('section', 'seq', 'mp')
Inputs may be any that keep to these rules, and one draw needn't show every extreme that they name: `queries`: rows drawn about normal; a layer's rows may differ in scale. `block_order`: A permutation of the position blocks.
All inputs are finite; a program needn't handle non-finite values.
Results may differ from a plain program's by a relative error of at most 0.035.
The roundings to bfloat16 on the way count: a program that leaves them out, or rounds other values in their place, can miss the bound.
Values may be sent and summed in bfloat16 or wider, within the bound.
A program may use at most 64 MiB of HBM per device.

v0:
```python
import jax
import jax.numpy as jnp
from jax import lax
from jax.sharding import PartitionSpec as P

HD = 128
SLOTS = 4


def contract_rows(left, right):
    return lax.dot_general(
        left, right, (((0,), (0,)), ((), ())), preferred_element_type=jnp.float32
    )


def contract_cols(left, right):
    return lax.dot_general(
        left, right, (((1,), (1,)), ((), ())), preferred_element_type=jnp.float32
    )


def place_rows(rows, block_order, half):
    slots = rows // half
    table = jnp.arange(block_order.shape[0], dtype=jnp.int32)
    match = slots[:, None] == table[None, :]
    first = jnp.sum(jnp.where(match, block_order[None, :], 0), axis=1)
    return first * half + rows % half


def body(rows40, queries, kv_weight, out_grad, block_order):
    scale = HD ** (-0.5)
    whole = lax.all_gather(rows40, ("section", "mp"), axis=1, tiled=True)
    weight_rows = kv_weight[0]
    tok_dev = whole.shape[0]
    seq_index = lax.axis_index("seq")
    half = tok_dev // SLOTS
    part = whole
    own_kv = jnp.dot(
        part,
        lax.all_gather(weight_rows, "seq", axis=0, tiled=True),
        preferred_element_type=jnp.float32,
    )
    all_kv = lax.all_gather(own_kv.astype(jnp.bfloat16), "seq", axis=0, tiled=True)
    group = queries.shape[2] // HD
    query_rows = queries[0].reshape(tok_dev * group, HD)
    grad_rows = out_grad[0].reshape(tok_dev * group, HD)
    rows_total = query_rows.shape[0]
    own_pos = place_rows(
        seq_index * tok_dev + jnp.arange(tok_dev, dtype=jnp.int32), block_order, half
    )
    query_pos = jnp.repeat(own_pos, group)
    key_len = all_kv.shape[0]
    block = min(512, key_len)
    blocks_total = key_len // block
    key_pos = place_rows(jnp.arange(key_len, dtype=jnp.int32), block_order, half).reshape(
        blocks_total, block
    )
    keys = all_kv[:, :HD].reshape(blocks_total, block, HD)
    values = all_kv[:, HD:].reshape(blocks_total, block, HD)

    def masked_scores(key_block, pos_block):
        raw = contract_cols(query_rows, key_block) * scale
        return jnp.where(pos_block[None, :] <= query_pos[:, None], raw, -1e30)

    def stats_step(state, blocks):
        key_block, pos_block = blocks
        peak, total = state
        scores = masked_scores(key_block, pos_block)
        new_peak = jnp.maximum(peak, jnp.max(scores, axis=1))
        total = total * jnp.exp(peak - new_peak) + jnp.sum(
            jnp.exp(scores - new_peak[:, None]), axis=1
        )
        return ((new_peak, total), None)

    start_state = (
        jnp.full((rows_total,), -1e30, jnp.float32),
        jnp.zeros((rows_total,), jnp.float32),
    )
    (peak, total), _ = lax.scan(stats_step, start_state, (keys, key_pos))

    def probabilities(key_block, pos_block):
        scores = masked_scores(key_block, pos_block)
        return jnp.exp(scores - peak[:, None]) / total[:, None]

    def output_step(accum, blocks):
        key_block, value_block, pos_block = blocks
        weights = probabilities(key_block, pos_block).astype(jnp.bfloat16)
        return (accum + jnp.dot(weights, value_block, preferred_element_type=jnp.float32), None)

    accum, _ = lax.scan(
        output_step, jnp.zeros((rows_total, HD), jnp.float32), (keys, values, key_pos)
    )
    attended = accum.astype(jnp.bfloat16)
    delta = jnp.sum(grad_rows.astype(jnp.float32) * attended.astype(jnp.float32), axis=1)

    def grad_step(dquery, blocks):
        key_block, value_block, pos_block = blocks
        probs = probabilities(key_block, pos_block)
        weights = probs.astype(jnp.bfloat16)
        dprob = contract_cols(grad_rows, value_block)
        dscore = (probs * (dprob - delta[:, None]) * scale).astype(jnp.bfloat16)
        new_dquery = dquery + jnp.dot(dscore, key_block, preferred_element_type=jnp.float32)
        dkey = contract_rows(dscore, query_rows)
        dvalue = contract_rows(weights, grad_rows)
        return (new_dquery, jnp.concatenate([dkey, dvalue], axis=1))

    dquery, key_terms = lax.scan(
        grad_step, jnp.zeros((rows_total, HD), jnp.float32), (keys, values, key_pos)
    )
    key_terms = key_terms.reshape(key_len, 2 * HD)
    own_grad = lax.psum_scatter(
        key_terms.astype(jnp.bfloat16), "seq", scatter_dimension=0, tiled=True
    )
    part = whole
    weight_grad = lax.psum_scatter(
        contract_rows(part, own_grad).astype(jnp.bfloat16), "seq", scatter_dimension=0, tiled=True
    ).astype(jnp.float32)
    attended_out = attended.reshape(1, tok_dev, group * HD)
    query_grad = dquery.astype(jnp.bfloat16).reshape(1, tok_dev, group * HD)
    return (attended_out, query_grad, weight_grad[None])


def solution(mesh):
    return jax.shard_map(
        body,
        mesh=mesh,
        in_specs=(
            P("seq", ("section", "mp")),
            P("section", "seq", "mp"),
            P("section", "seq", "mp"),
            P("section", "seq", "mp"),
            P(),
        ),
        out_specs=(P("section", "seq", "mp"), P("section", "seq", "mp"), P("section", "seq", "mp")),
        check_vma=False,
    )
```

profile of v0, /device:TPU:1, one launch (start us, length us, event | category | flops | bytes accessed | tf_op | source)
XLA Modules:
  0.0 511.5 jit_solution(14380077282246239146)
XLA Ops:
  7.9 0.7 all-gather.9.cloned.1.call-update
  8.7 89.5 %all-gather.5.cloned.1.call-done = bf16[192,8192]{1,0:T(8,128)(2,1)} async-done(((bf16[192,512]{1,0:T(8,128)(2,1)}), bf16[192,8192]{1,0:T(8,128)(2,1)}) %all-gather.5.cloned.1.call-update) | async-done | bytes 3145744 | tf_op jit(solution)/shard_map/all_gather | solution.py:32
  98.2 86.2 %all-gather.9.cloned.1.call-done = bf16[1,8192,256]{2,1,0:T(8,128)(2,1)} async-done(((bf16[1,512,256]{2,1,0:T(8,128)(2,1)}), bf16[1,8192,256]{2,1,0:T(8,128)(2,1)}) %all-gather.9.cloned.1.call-update) | async-done | bytes 4194320 | tf_op jit(solution)/shard_map/all_gather | solution.py:40
  184.4 4.8 fusion.49
  190.1 54.1 %all-gather.7.cloned.1.call-done = bf16[3072,256]{1,0:T(8,128)(2,1)} async-done(((bf16[192,256]{1,0:T(8,128)(2,1)}), bf16[3072,256]{1,0:T(8,128)(2,1)}) %all-gather.7.cloned.1.call-update) | async-done | bytes 1572880 | tf_op jit(solution)/shard_map/all_gather | solution.py:43
  244.2 2.3 fusion.63
  246.6 13.6 %while.37 = (s32[]{:T(128)}, f32[1536]{0:T(1024)S(1)}, f32[1536]{0:T(1024)S(1)}, s32[6,512]{1,0:T(8,128)S(1)}, bf16[6,512,128]{2,1,0:T(8,128)(2,1)}, /*index=5*/...) while((s32[]{:T(128)}, f32[1536]{0:T(1024)S(1)}, f32[1536]{0:T(1024)S(1)}, ...), condition=%wide.region_5.6_spmd.clone, body=%wide.region_2.5_spmd.clone.sunk | while | flops 206052864 | bytes 6927224 | solution.py:79
  246.8 1.5 fusion.97
  249.0 1.5 fusion.97
  251.3 1.5 fusion.97
  253.6 1.5 fusion.97
  255.8 1.5 fusion.97
  258.1 1.5 fusion.97
  260.1 16.3 %while.38 = (s32[]{:T(128)}, f32[1536,128]{1,0:T(8,128)S(1)}, s32[6,512]{1,0:T(8,128)S(1)}, bf16[6,512,128]{2,1,0:T(8,128)(2,1)}, bf16[1536,128]{1,0:T(8,128)(2,...) while((s32[]{:T(128)}, f32[1536,128]{1,0:T(8,128)S(1)}, ...), condition=%wide.region_7.8_spmd.clone, body=%wide.region_6.7_spmd.clone.sunk | while | flops 407764992 | bytes 2279810 | solution.py:90
  260.4 2.5 convolution_add_fusion.4
  263.1 2.5 convolution_add_fusion.4
  265.8 2.5 convolution_add_fusion.4
  268.5 2.5 convolution_add_fusion.4
  271.3 2.5 convolution_add_fusion.4
  274.0 2.5 convolution_add_fusion.4
  276.5 0.9 copy-done
  277.4 1.4 multiply_reduce_fusion
  278.8 40.4 %while.39 = (s32[]{:T(128)}, f32[1536,128]{1,0:T(8,128)S(1)}, bf16[6,512,256]{2,1,0:T(8,128)(2,1)}, s32[6,512]{1,0:T(8,128)S(1)}, bf16[6,512,128]{2,1,0:T(8,128)...) while((s32[]{:T(128)}, f32[1536,128]{1,0:T(8,128)S(1)}, ...), condition=%wide.region_10.11_spmd.clone, body=%wide.region_9.10_spmd.clone.sunk | while | flops 1015414784 | bytes 19581868 | solution.py:107
  279.0 1.9 fusion.112
  282.8 1.8 convolution_add_fusion.5
  284.8 0.7 constant_dynamic-update-slice_fusion.2
  285.7 1.9 fusion.112
  289.5 1.8 convolution_add_fusion.5
  291.5 0.7 constant_dynamic-update-slice_fusion.2
  292.5 1.9 fusion.112
  296.3 1.8 convolution_add_fusion.5
  298.3 0.7 constant_dynamic-update-slice_fusion.2
  299.2 1.9 fusion.112
  303.0 1.8 convolution_add_fusion.5
  305.0 0.7 constant_dynamic-update-slice_fusion.2
  305.9 1.8 fusion.112
  309.7 1.8 convolution_add_fusion.5
  311.7 0.7 constant_dynamic-update-slice_fusion.2
  312.6 1.8 fusion.112
  316.4 1.8 convolution_add_fusion.5
  318.4 0.7 constant_dynamic-update-slice_fusion.2
  319.3 77.6 %reduce-scatter.3.cloned.1.call-done = bf16[192,256]{1,0:T(8,128)(2,1)} async-done(((bf16[3072,256]{1,0:T(8,128)(2,1)}), bf16[192,256]{1,0:T(8,128)(2,1)}) %reduce-scatter.3.cloned.1.call-update) | async-done | bytes 98320 | tf_op jit(solution)/shard_map/reduce_scatter | solution.py:111
  396.9 5.2 %fusion.46 = bf16[8192,256]{0,1:T(8,128)(2,1)} fusion(bf16[192,256]{1,0:T(8,128)(2,1)} %reduce-scatter.3.cloned.1.call-done, bf16[192,8192]{1,0:T(8,128)(2,1)} %all-gather.5.cloned.1.call-done), kind=kOutput, calls=%fused_computation.56 | convolution fusion | flops 807403520 | bytes 7438336 | tf_op jit(solution)/shard_map/dot_general | solution.py:11
  402.1 0.9 reshape.62
  403.0 0.9 reshape.63
  403.9 99.0 %reduce-scatter.5.cloned.1.call-done = bf16[512,256]{0,1:T(8,128)(2,1)} async-done(((bf16[8192,256]{0,1:T(8,128)(2,1)}), bf16[512,256]{0,1:T(8,128)(2,1)}) %reduce-scatter.5.cloned.1.call-update) | async-done | bytes 262160 | tf_op jit(solution)/shard_map/reduce_scatter | solution.py:115
  503.0 1.0 bitcast_convert_fusion
  504.0 1.0 copy.12
  (140 shorter events, 20.5 us)
Async XLA Ops:
  7.2 91.1 %all-gather.5.cloned.1.call-start = ((), (), s32[]{:S(2)}) async-start(), calls=%async_computation.2 | async-start | bytes 3342336 | tf_op jit(solution)/shard_map/all_gather | solution.py:32
  7.9 176.5 %all-gather.9.cloned.1.call-start = ((), (), s32[]{:S(2)}) async-start(), calls=%async_computation.6 | async-start | bytes 4456448 | tf_op jit(solution)/shard_map/all_gather | solution.py:40
  8.6 180.7 %copy-start.3 = (s32[64]{0:T(128)S(1)}, s32[64]{0:T(128)}, u32[]{:S(2)}) copy-start(s32[64]{0:T(128)} %param.15) | copy-start | bytes 772
  8.7 180.9 %copy-start.1 = (bf16[1,192,1024]{2,1,0:T(8,128)(2,1)S(1)}, bf16[1,192,1024]{2,1,0:T(8,128)(2,1)}, u32[]{:S(2)}) copy-start(bf16[1,192,1024]{2,1,0:T(8,128)(2,1)} %param.12) | copy-start | bytes 1179652
  8.7 181.1 %copy-start.2 = (bf16[1,192,1024]{2,1,0:T(8,128)(2,1)S(1)}, bf16[1,192,1024]{2,1,0:T(8,128)(2,1)}, u32[]{:S(2)}) copy-start(bf16[1,192,1024]{2,1,0:T(8,128)(2,1)} %param.14) | copy-start | bytes 1179652
  8.7 235.5 %all-gather.7.cloned.1.call-start = ((), (), s32[]{:S(2)}) async-start(), calls=%async_computation.3 | async-start | bytes 1671168 | tf_op jit(solution)/shard_map/all_gather | solution.py:43
  189.2 207.6 %reduce-scatter.3.cloned.1.call-start = ((), (), s32[]{:S(2)}) async-start(), calls=%async_computation.4 | async-start | bytes 1671168 | tf_op jit(solution)/shard_map/reduce_scatter | solution.py:111
  276.5 0.9 copy-start
  319.2 183.8 %reduce-scatter.5.cloned.1.call-start = ((), (), s32[]{:S(2)}) async-start(), calls=%async_computation.5 | async-start | bytes 4456448 | tf_op jit(solution)/shard_map/reduce_scatter | solution.py:115
Sparse Core Ops, SparseCore 0:
  9.8 88.4 all-gather.4
  100.9 83.4 all-gather.8
  189.3 54.8 all-gather.6
  319.3 77.4 reduce-scatter.2
  402.2 100.7 reduce-scatter.4
where the time goes:
time: 513 us; the launch traced here: 512 us
  waiting for transfers between devices  408 us (80%)
  matrix products  67.4 us (13%)
  local copies, waits for them, and re-layouts  15 us (3%)
  between operations  14 us (3%)
  other arithmetic  5.93 us (1%)
    reduce_scatter x1, waiting for transfers between devices, body(): lax.psum_scatter(contract_rows(part, own_grad).astype(jnp.bfloat16), 'seq...  99 us
    all_gather x1, waiting for transfers between devices, body(): whole = lax.all_gather(rows40, ('section', 'mp'), axis=1, tiled=True)  89.5 us
    all_gather x1, waiting for transfers between devices, body(): lax.all_gather(weight_rows, 'seq', axis=0, tiled=True)  86.2 us
    reduce_scatter x1, waiting for transfers between devices, body(): lax.psum_scatter(key_terms.astype(jnp.bfloat16), 'seq', scatter_dimension...  77.6 us
    all_gather x1, waiting for transfers between devices, body(): lax.all_gather(own_kv.astype(jnp.bfloat16), 'seq', axis=0, tiled=True)  54.1 us
    dot_general x18, matrix products, contract_cols(): lax.dot_general(left, right, (((1,), (1,)), ((), ())), preferred_element_...  23.6 us
    dot_general x6, matrix products, output_step(): jnp.dot(weights, value_block, preferred_element_type=jnp.float32)  14.9 us
    dot_general x13, matrix products, contract_rows(): lax.dot_general(left, right, (((0,), (0,)), ((), ())), preferred_element_...  13.1 us
  transfers between devices with their start and end apart: 5, of which 5 were waited for; matrix products, arithmetic and copies ran while one was open for 1% of the time, Pallas kernels for 0%

commit v1 on v0

v1 whole, which is shorter than its diff:
```python
import functools

import jax
import jax.numpy as jnp
from jax import lax
import jax.experimental.pallas as pl
import jax.experimental.pallas.tpu as pltpu
from jax.sharding import PartitionSpec as P

HD = 128
SLOTS = 4
CHUNK = 256
VMEM_LIMIT = 60 * 2**20
MESH = pl.DeviceIdType.MESH
LOG2E = 1.4426950408889634


def contract(left, right, left_dim, right_dim):
    return lax.dot_general(
        left,
        right,
        (((left_dim,), (right_dim,)), ((), ())),
        preferred_element_type=jnp.float32,
    )


class Copies:
    def __init__(self, send_sem, recv_sem):
        self.send_sem = send_sem
        self.recv_sem = recv_sem
        self.count = 0
        self.started = []

    def slot(self):
        self.count += 1
        return self.count - 1

    def make(self, slot, src, dst, device):
        return pltpu.make_async_remote_copy(
            src_ref=src,
            dst_ref=dst,
            send_sem=self.send_sem.at[slot],
            recv_sem=self.recv_sem.at[slot],
            device_id=device,
            device_id_type=MESH,
        )

    def start(self, slot, src, dst, device):
        copy = self.make(slot, src, dst, device)
        copy.start()
        self.started.append(copy)

    def wait_recv(self, slot, buf, device):
        self.make(slot, buf, buf, device).wait_recv()

    def finish(self):
        for copy in self.started:
            copy.wait_send()


def place():
    sec = lax.axis_index("section")
    seq = lax.axis_index("seq")
    mp = lax.axis_index("mp")
    return sec, seq, mp


def greet(peers):
    barrier = pltpu.get_barrier_semaphore()
    for peer in peers:
        pl.semaphore_signal(barrier, inc=1, device_id=peer, device_id_type=MESH)
    pl.semaphore_wait(barrier, len(peers))


def seq_peers(sec, seq, mp):
    zhi = lax.rem(seq // 2, 2)
    core = lax.rem(seq, 2)
    across = (sec, seq + 2 - 4 * zhi, mp)
    other = (sec, seq + 1 - 2 * core, mp)
    along = {d: (sec, lax.rem(seq + 4 * d, 16), mp) for d in (1, 2, 3)}
    return across, other, along


class SeqGather:
    def __init__(self, copies, buf, sec, seq, mp):
        self.copies = copies
        self.buf = buf
        self.seq = seq
        self.across, self.other, self.along = seq_peers(sec, seq, mp)
        self.z_slot = copies.slot()
        self.y_slot = {(t, d): copies.slot() for t in (0, 1) for d in (1, 2, 3)}
        self.c_slot = {(t, d): copies.slot() for t in (0, 1) for d in (0, 1, 2, 3)}

    def index(self, t, d):
        own = lax.rem(self.seq + 16 - 4 * d, 16)
        if t == 0:
            return own
        return own + 2 - 4 * lax.rem(own // 2, 2)

    def send(self, slot, t, d, device):
        block = self.buf.at[self.index(t, d)]
        self.copies.start(slot, block, block, device)

    def begin(self):
        self.send(self.z_slot, 0, 0, self.across)
        for d in (1, 2, 3):
            self.send(self.y_slot[0, d], 0, 0, self.along[d])
        self.send(self.c_slot[0, 0], 0, 0, self.other)

    def relay_across(self):
        self.copies.wait_recv(self.z_slot, self.buf.at[0], self.across)
        for d in (1, 2, 3):
            self.send(self.y_slot[1, d], 1, 0, self.along[d])
        self.send(self.c_slot[1, 0], 1, 0, self.other)

    def relay_core(self, t, d):
        self.copies.wait_recv(self.y_slot[t, d], self.buf.at[0], self.along[d])
        self.send(self.c_slot[t, d], t, d, self.other)

    def end(self):
        for t in (0, 1):
            for d in (0, 1, 2, 3):
                self.copies.wait_recv(self.c_slot[t, d], self.buf.at[0], self.other)


def project_kernel(rows_ref, weight_ref, kv_ref, rows_all, weight_all, send_sem, recv_sem):
    sec, seq, mp = place()
    copies = Copies(send_sem, recv_sem)
    mp_peer = {d: (sec, seq, lax.rem(mp + d, 4)) for d in (1, 2, 3)}
    sec_peer = {d: (lax.rem(sec + d, 4), seq, mp) for d in (1, 2, 3)}
    across, other, along = seq_peers(sec, seq, mp)
    greet(
        [mp_peer[d] for d in (1, 2, 3)]
        + [sec_peer[d] for d in (1, 2, 3)]
        + [along[d] for d in (1, 2, 3)]
        + [across, other]
    )
    own = sec * 4 + mp
    rows_all[own] = rows_ref[...]
    weight_all[seq] = weight_ref[0]
    gather_w = SeqGather(copies, weight_all, sec, seq, mp)
    m_slot = {d: copies.slot() for d in (1, 2, 3)}
    x_slot = {(e, d): copies.slot() for e in (0, 1, 2, 3) for d in (1, 2, 3)}

    for d in (1, 2, 3):
        copies.start(m_slot[d], rows_all.at[own], rows_all.at[own], mp_peer[d])
    gather_w.begin()
    for d in (1, 2, 3):
        copies.start(x_slot[0, d], rows_all.at[own], rows_all.at[own], sec_peer[d])
    for e in (1, 3, 2):
        copies.wait_recv(m_slot[e], rows_all.at[0], mp_peer[e])
        block = sec * 4 + lax.rem(mp + 4 - e, 4)
        for d in (1, 2, 3):
            copies.start(x_slot[e, d], rows_all.at[block], rows_all.at[block], sec_peer[d])
        if e == 1:
            gather_w.relay_across()
    for t in (0, 1):
        for d in (1, 3, 2):
            gather_w.relay_core(t, d)
    for e in (0, 1, 3, 2):
        for d in (1, 3, 2):
            copies.wait_recv(x_slot[e, d], rows_all.at[0], sec_peer[d])
    gather_w.end()

    def term(f, total):
        return total + jnp.dot(
            rows_all[f], weight_all[f], preferred_element_type=jnp.float32
        )

    total = lax.fori_loop(0, 16, term, jnp.zeros(kv_ref.shape[1:], jnp.float32))
    kv_ref[seq] = total.astype(kv_ref.dtype)

    gather_kv = SeqGather(copies, kv_ref, sec, seq, mp)
    gather_kv.begin()
    gather_kv.relay_core(0, 1)
    gather_kv.relay_core(0, 3)
    gather_kv.relay_core(0, 2)
    gather_kv.relay_across()
    for d in (1, 3, 2):
        gather_kv.relay_core(1, d)
    gather_kv.end()
    copies.finish()


def project(rows, weight):
    tok, feat = rows.shape
    cols = weight.shape[2]
    sems = 45
    return pl.pallas_call(
        project_kernel,
        out_shape=jax.ShapeDtypeStruct((16, tok, cols), jnp.bfloat16),
        in_specs=[pl.BlockSpec(memory_space=pltpu.VMEM)] * 2,
        out_specs=pl.BlockSpec(memory_space=pltpu.VMEM),
        scratch_shapes=[
            pltpu.VMEM((16, tok, feat), jnp.bfloat16),
            pltpu.VMEM((16, feat, cols), jnp.bfloat16),
            pltpu.SemaphoreType.DMA((sems,)),
            pltpu.SemaphoreType.DMA((sems,)),
        ],
        compiler_params=pltpu.CompilerParams(
            collective_id=0, has_side_effects=True, vmem_limit_bytes=VMEM_LIMIT
        ),
        name="project",
    )(rows, weight)


def attention_kernel(
    order, q_ref, g_ref, kv_ref, att_ref, dq_ref, dkv_ref, kv_pos, kv_t, acc, score, prob
):
    seq = lax.axis_index("seq")
    half = q_ref.shape[0] // SLOTS
    group = q_ref.shape[1] // HD
    keys = kv_ref.shape[0]
    lanes = group * half
    scale = HD ** (-0.5)
    rate = scale * LOG2E

    def rows_at(start, size):
        return pl.ds(pl.multiple_of(start, 16), size)

    def by_position(r, carry):
        kv_pos[rows_at(order[r] * half, half), :] = kv_ref[rows_at(r * half, half), :]
        return carry

    lax.fori_loop(0, keys // half, by_position, 0)

    def turn(j, carry):
        kv_t[j] = kv_pos[rows_at(j * CHUNK, CHUNK), :].T
        acc[rows_at(j * CHUNK, CHUNK), :] = jnp.zeros((CHUNK, 2 * HD), jnp.float32)
        return carry

    lax.fori_loop(0, keys // CHUNK, turn, 0)

    def slot(i, carry):
        first = order[seq * SLOTS + i] * half
        rows = rows_at(i * half, half)
        q = jnp.concatenate([q_ref[rows, h * HD : (h + 1) * HD] for h in range(group)], axis=0)
        g = jnp.concatenate([g_ref[rows, h * HD : (h + 1) * HD] for h in range(group)], axis=0)
        whole = first // CHUNK
        some = (first + half + CHUNK - 1) // CHUNK

        def scores(masked):
            def step(j, peak):
                raw = contract(kv_pos[rows_at(j * CHUNK, CHUNK), :HD], q, 1, 1)
                if masked:
                    key = j * CHUNK + lax.broadcasted_iota(jnp.int32, raw.shape, 0)
                    query = first + lax.rem(
                        lax.broadcasted_iota(jnp.int32, raw.shape, 1), half
                    )
                    raw = jnp.where(key <= query, raw, -1e30)
                score[rows_at(j * CHUNK, CHUNK), :] = raw
                return jnp.maximum(peak, jnp.max(raw.reshape(CHUNK // 8, 8, lanes), axis=0))

            return step

        peak = jnp.full((8, lanes), -1e30, jnp.float32)
        peak = lax.fori_loop(0, whole, scores(False), peak)
        peak = lax.fori_loop(whole, some, scores(True), peak)
        peak = jnp.max(peak, axis=0, keepdims=True)

        def weigh(j, total):
            at = rows_at(j * CHUNK, CHUNK)
            expo = jnp.exp2((score[at, :] - peak) * rate)
            score[at, :] = expo
            return total + jnp.sum(expo.reshape(CHUNK // 8, 8, lanes), axis=0)

        total = lax.fori_loop(0, some, weigh, jnp.zeros((8, lanes), jnp.float32))
        part = 1.0 / jnp.sum(total, axis=0, keepdims=True)

        def attend(j, out):
            at = rows_at(j * CHUNK, CHUNK)
            weights = (score[at, :] * part).astype(jnp.bfloat16)
            prob[at, :] = weights
            return out + jnp.dot(kv_t[j, HD:], weights, preferred_element_type=jnp.float32)

        out = lax.fori_loop(0, some, attend, jnp.zeros((HD, lanes), jnp.float32))
        out = out.astype(jnp.bfloat16).astype(jnp.float32)
        delta = jnp.sum(g.astype(jnp.float32).T * out, axis=0, keepdims=True)
        out = out.T.astype(jnp.bfloat16)
        for h in range(group):
            att_ref[rows, h * HD : (h + 1) * HD] = out[h * half : (h + 1) * half, :]
        part_scaled = part * scale

        def back(j, dquery):
            at = rows_at(j * CHUNK, CHUNK)
            dprob = contract(kv_pos[at, HD:], g, 1, 1)
            dscore = (score[at, :] * part_scaled * (dprob - delta)).astype(jnp.bfloat16)
            acc[at, :HD] += jnp.dot(dscore, q, preferred_element_type=jnp.float32)
            acc[at, HD:] += jnp.dot(prob[at, :], g, preferred_element_type=jnp.float32)
            return dquery + jnp.dot(kv_t[j, :HD], dscore, preferred_element_type=jnp.float32)

        dquery = lax.fori_loop(0, some, back, jnp.zeros((HD, lanes), jnp.float32))
        dquery = dquery.T.astype(jnp.bfloat16)
        for h in range(group):
            dq_ref[rows, h * HD : (h + 1) * HD] = dquery[h * half : (h + 1) * half, :]
        return carry

    lax.fori_loop(0, SLOTS, slot, 0)

    def by_token(r, carry):
        dkv_ref[rows_at(r * half, half), :] = acc[rows_at(order[r] * half, half), :].astype(
            jnp.bfloat16
        )
        return carry

    lax.fori_loop(0, keys // half, by_token, 0)


def attention(order, queries, out_grad, kv):
    tok, cols = queries.shape
    keys = kv.shape[0]
    lanes = cols // HD * (tok // SLOTS)
    vmem = pl.BlockSpec(memory_space=pltpu.VMEM)
    return pl.pallas_call(
        attention_kernel,
        out_shape=(
            jax.ShapeDtypeStruct((tok, cols), jnp.bfloat16),
            jax.ShapeDtypeStruct((tok, cols), jnp.bfloat16),
            jax.ShapeDtypeStruct((keys, 2 * HD), jnp.bfloat16),
        ),
        in_specs=[pl.BlockSpec(memory_space=pltpu.SMEM), vmem, vmem, vmem],
        out_specs=(vmem, vmem, vmem),
        scratch_shapes=[
            pltpu.VMEM((keys, 2 * HD), jnp.bfloat16),
            pltpu.VMEM((keys // CHUNK, 2 * HD, CHUNK), jnp.bfloat16),
            pltpu.VMEM((keys, 2 * HD), jnp.float32),
            pltpu.VMEM((keys, lanes), jnp.float32),
            pltpu.VMEM((keys, lanes), jnp.bfloat16),
        ],
        compiler_params=pltpu.CompilerParams(vmem_limit_bytes=VMEM_LIMIT),
        name="attention",
    )(order, queries, out_grad, kv)


def weight_grad_kernel(
    rows_ref, dkv_ref, out_ref, rows_t, core_in, y_out, y_in, z_out, z_in, grad, send_sem, recv_sem
):
    sec, seq, mp = place()
    copies = Copies(send_sem, recv_sem)
    yy = seq // 4
    core = lax.rem(seq, 2)
    across, other, along = seq_peers(sec, seq, mp)
    sec_peer = {d: (lax.rem(sec + d, 4), seq, mp) for d in (1, 2, 3)}
    feature = sec * 4 + mp
    diagonal = seq == feature
    to_peer = {d: (seq // 4, feature, lax.rem(mp + d, 4)) for d in (0, 1, 2, 3)}
    from_peer = {j: (seq // 4, sec * 4 + j, lax.rem(seq, 4)) for j in (0, 1, 2, 3)}

    barrier = pltpu.get_barrier_semaphore()
    fixed = [sec_peer[d] for d in (1, 2, 3)] + [along[d] for d in (1, 2, 3)] + [across, other]
    for peer in fixed:
        pl.semaphore_signal(barrier, inc=1, device_id=peer, device_id_type=MESH)
    for j in (0, 1, 2, 3):
        away = jnp.logical_not(jnp.logical_and(diagonal, mp == j))

        @pl.when(away)
        def _():
            pl.semaphore_signal(barrier, inc=1, device_id=from_peer[j], device_id_type=MESH)

    pl.semaphore_wait(barrier, len(fixed) + 4 - diagonal.astype(jnp.int32))

    first_slot = [copies.slot() for _ in range(4)]
    x_slot = {(j, d): copies.slot() for j in range(4) for d in (1, 2, 3)}
    core_slot = [copies.slot() for _ in range(4)]
    y_slot = {d: copies.slot() for d in (1, 2, 3)}
    z_slot = copies.slot()
    ag_slot = {d: copies.slot() for d in (1, 2, 3)}
    cg_slot = {d: copies.slot() for d in (0, 1, 2, 3)}

    for d in (1, 2, 3, 0):
        yt = lax.rem(yy + d, 4)
        copies.start(core_slot[d], dkv_ref.at[yt, :, 1 - core], core_in.at[d], other)

    def first_copy(d):
        return pltpu.make_async_remote_copy(
            src_ref=rows_ref,
            dst_ref=rows_t.at[seq],
            send_sem=send_sem.at[first_slot[d]],
            recv_sem=recv_sem.at[first_slot[0] + lax.rem(seq, 4)],
            device_id=to_peer[d],
            device_id_type=MESH,
        )

    for d in (1, 2, 3):
        first_copy(d).start()

    @pl.when(diagonal)
    def _():
        rows_t[seq] = rows_ref[...]

    @pl.when(jnp.logical_not(diagonal))
    def _():
        first_copy(0).start()

    for d in (1, 2, 3):
        yt = lax.rem(yy + d, 4)
        copies.wait_recv(core_slot[d], core_in.at[d], other)
        y_out[d - 1] = (
            dkv_ref[yt, :, core].astype(jnp.float32) + core_in[d].astype(jnp.float32)
        ).astype(jnp.bfloat16)
        copies.start(y_slot[d], y_out.at[d - 1], y_in.at[d - 1], along[d])
    copies.wait_recv(core_slot[0], core_in.at[0], other)

    for j in range(4):
        @pl.when(jnp.logical_not(jnp.logical_and(diagonal, mp == j)))
        def _():
            copies.wait_recv(first_slot[j], rows_t.at[0], from_peer[j])

        block = rows_t.at[sec * 4 + j]
        for d in (1, 2, 3):
            copies.start(x_slot[j, d], block, block, sec_peer[d])

    for d in (1, 2, 3):
        copies.wait_recv(y_slot[d], y_in.at[d - 1], along[d])
    z_out[...] = (
        dkv_ref[yy, :, core].astype(jnp.float32)
        + core_in[0].astype(jnp.float32)
        + y_in[0].astype(jnp.float32)
        + y_in[1].astype(jnp.float32)
        + y_in[2].astype(jnp.float32)
    ).astype(jnp.bfloat16)
    copies.start(z_slot, z_out, z_in, across)
    copies.wait_recv(z_slot, z_in, across)
    grad[yy, :, core] = (
        z_out[...].astype(jnp.float32) + z_in[...].astype(jnp.float32)
    ).astype(jnp.bfloat16)
    own = grad.at[yy, :, core]
    for d in (1, 2, 3):
        copies.start(ag_slot[d], own, own, along[d])
    copies.start(cg_slot[0], own, own, other)
    for d in (1, 3, 2):
        block = grad.at[lax.rem(yy + 4 - d, 4), :, core]
        copies.wait_recv(ag_slot[d], block, along[d])
        copies.start(cg_slot[d], block, block, other)
    for d in (0, 1, 3, 2):
        copies.wait_recv(cg_slot[d], grad.at[0, :, 0], other)
    for j in range(4):
        for d in (1, 3, 2):
            copies.wait_recv(x_slot[j, d], rows_t.at[0], sec_peer[d])

    out_ref[...] = jnp.zeros_like(out_ref)

    def term(t, carry):
        block = grad[t // 4, lax.rem(t // 2, 2), lax.rem(t, 2)]
        out_ref[...] += contract(rows_t[t], block, 0, 0)
        return carry

    lax.fori_loop(0, 16, term, 0)

    for d in (1, 2, 3):
        first_copy(d).wait_send()

    @pl.when(jnp.logical_not(diagonal))
    def _():
        first_copy(0).wait_send()

    copies.finish()


def weight_grad(rows, dkv):
    tok, feat = rows.shape
    cols = dkv.shape[1]
    sems = 40
    vmem = pl.BlockSpec(memory_space=pltpu.VMEM)
    half = (2, tok, cols)
    return pl.pallas_call(
        weight_grad_kernel,
        out_shape=jax.ShapeDtypeStruct((feat, cols), jnp.float32),
        in_specs=[vmem, vmem],
        out_specs=vmem,
        scratch_shapes=[
            pltpu.VMEM((16, tok, feat), jnp.bfloat16),
            pltpu.VMEM((4,) + half, jnp.bfloat16),
            pltpu.VMEM((3,) + half, jnp.bfloat16),
            pltpu.VMEM((3,) + half, jnp.bfloat16),
            pltpu.VMEM(half, jnp.bfloat16),
            pltpu.VMEM(half, jnp.bfloat16),
            pltpu.VMEM((4, 2, 2, tok, cols), jnp.bfloat16),
            pltpu.SemaphoreType.DMA((sems,)),
            pltpu.SemaphoreType.DMA((sems,)),
        ],
        compiler_params=pltpu.CompilerParams(
            collective_id=1, has_side_effects=True, vmem_limit_bytes=VMEM_LIMIT
        ),
        name="weight_grad",
    )(rows, dkv.reshape(4, 2, 2, tok, cols))


def body(rows40, queries, kv_weight, out_grad, block_order):
    tok = rows40.shape[0]
    kv = project(rows40, kv_weight)
    attended, query_grad, dkv = attention(
        block_order, queries[0], out_grad[0], kv.reshape(16 * tok, 2 * HD)
    )
    grad = weight_grad(rows40, dkv)
    return (attended[None], query_grad[None], grad[None])


def solution(mesh):
    return jax.shard_map(
        body,
        mesh=mesh,
        in_specs=(
            P("seq", ("section", "mp")),
            P("section", "seq", "mp"),
            P("section", "seq", "mp"),
            P("section", "seq", "mp"),
            P(),
        ),
        out_specs=(P("section", "seq", "mp"), P("section", "seq", "mp"), P("section", "seq", "mp")),
        check_vma=False,
    )
```

time: 513 us -> 208 us (0.41)
  the two profiles are of different devices: /device:TPU:1 before, /device:TPU:97 now
where the time goes in v1:
time: 208 us; the launch traced here: 207 us
  Pallas kernels  205 us (99%)
    pallas_call x1, Pallas kernels, weight_grad(): pl.pallas_call(weight_grad_kernel, out_shape=jax.ShapeDtypeStruct((feat,...  84 us
    pallas_call x1, Pallas kernels, project(): pl.pallas_call(project_kernel, out_shape=jax.ShapeDtypeStruct((16, tok, c...  72.2 us
    pallas_call x1, Pallas kernels, attention(): pl.pallas_call(attention_kernel, out_shape=(jax.ShapeDtypeStruct((tok, co...  48.7 us

profile of v1, /device:TPU:97, one launch (start us, length us, event | category | flops | bytes accessed | tf_op | source)
XLA Modules:
  0.0 207.4 jit_solution(6812761636735318070)
XLA Ops:
  0.6 72.2 %project.1 = bf16[16,192,256]{2,1,0:T(8,128)(2,1)} custom-call(bf16[192,512]{1,0:T(8,128)(2,1)} %rows_ref.3, bf16[1,512,256]{2,1,0:T(8,128)(2,1)} %weight_ref.1), custom_call_target="tpu_custom_call" | custom-call | tf_op jit(solution)/shard_map/project/pallas_call | solution.py:189
  72.9 48.7 %attention.1 = (bf16[192,1024]{1,0:T(8,128)(2,1)}, bf16[192,1024]{1,0:T(8,128)(2,1)}, bf16[3072,256]{1,0:T(8,128)(2,1)}) custom-call(s32[64]{0:T(128)} %order.1, bf16[192,1024]{1,0:T(8,128)(2,1)} %bitcast.10, bf16[192,1024]{1,0:T(8,128)(2,1)} %bitcast.11, bf16[3072,256]{1,0:T(8,128)(2,1)} %bitcast.7), custom_call_target="tpu_custom_call" | custom-call | tf_op jit(solution)/shard_map/attention/pallas_call | solution.py:314
  121.6 84.0 %weight_grad.1 = f32[512,256]{1,0:T(8,128)} custom-call(bf16[192,512]{1,0:T(8,128)(2,1)} %rows_ref.3, bf16[4,2,2,192,256]{4,3,2,1,0:T(8,128)(2,1)} %bitcast.9), custom_call_target="tpu_custom_call" | custom-call | tf_op jit(solution)/shard_map/weight_grad/pallas_call | solution.py:466
  205.6 1.9 copy.9

commit v2 on v1

v2 whole, which is shorter than its diff:
```python
import functools

import jax
import jax.numpy as jnp
from jax import lax
import jax.experimental.pallas as pl
import jax.experimental.pallas.tpu as pltpu
from jax.sharding import PartitionSpec as P

HD = 128
SLOTS = 4
PIECES = 4
VMEM_LIMIT = 60 * 2**20
MESH = pl.DeviceIdType.MESH
LOG2E = 1.4426950408889634


def contract(left, right, left_dim, right_dim):
    return lax.dot_general(
        left,
        right,
        (((left_dim,), (right_dim,)), ((), ())),
        preferred_element_type=jnp.float32,
    )


class Copies:
    def __init__(self, send_sem, recv_sem):
        self.send_sem = send_sem
        self.recv_sem = recv_sem
        self.count = 0
        self.started = []

    def slot(self):
        self.count += 1
        return self.count - 1

    def make(self, slot, src, dst, device):
        return pltpu.make_async_remote_copy(
            src_ref=src,
            dst_ref=dst,
            send_sem=self.send_sem.at[slot],
            recv_sem=self.recv_sem.at[slot],
            device_id=device,
            device_id_type=MESH,
        )

    def start(self, slot, src, dst, device):
        copy = self.make(slot, src, dst, device)
        copy.start()
        self.started.append(copy)

    def wait_recv(self, slot, buf, device):
        self.make(slot, buf, buf, device).wait_recv()

    def finish(self):
        for copy in self.started:
            copy.wait_send()


def place():
    sec = lax.axis_index("section")
    seq = lax.axis_index("seq")
    mp = lax.axis_index("mp")
    return sec, seq, mp


def greet(peers):
    barrier = pltpu.get_barrier_semaphore()
    for peer in peers:
        pl.semaphore_signal(barrier, inc=1, device_id=peer, device_id_type=MESH)
    pl.semaphore_wait(barrier, len(peers))


def seq_peers(sec, seq, mp):
    zhi = lax.rem(seq // 2, 2)
    core = lax.rem(seq, 2)
    across = (sec, seq + 2 - 4 * zhi, mp)
    other = (sec, seq + 1 - 2 * core, mp)
    along = {d: (sec, lax.rem(seq + 4 * d, 16), mp) for d in (1, 2, 3)}
    return across, other, along


class SeqGather:
    def __init__(self, copies, buf, sec, seq, mp):
        self.copies = copies
        self.buf = buf
        self.seq = seq
        self.across, self.other, self.along = seq_peers(sec, seq, mp)
        self.z_slot = copies.slot()
        self.y_slot = {(t, d): copies.slot() for t in (0, 1) for d in (1, 2, 3)}
        self.c_slot = {(t, d): copies.slot() for t in (0, 1) for d in (0, 1, 2, 3)}

    def index(self, t, d):
        own = lax.rem(self.seq + 16 - 4 * d, 16)
        if t == 0:
            return own
        return own + 2 - 4 * lax.rem(own // 2, 2)

    def send(self, slot, t, d, device):
        block = self.buf.at[self.index(t, d)]
        self.copies.start(slot, block, block, device)

    def begin_far(self):
        self.send(self.z_slot, 0, 0, self.across)

    def begin_near(self):
        for d in (1, 3, 2):
            self.send(self.y_slot[0, d], 0, 0, self.along[d])
        self.send(self.c_slot[0, 0], 0, 0, self.other)

    def relay_across(self):
        self.copies.wait_recv(self.z_slot, self.buf.at[0], self.across)
        for d in (1, 3, 2):
            self.send(self.y_slot[1, d], 1, 0, self.along[d])
        self.send(self.c_slot[1, 0], 1, 0, self.other)

    def relay_core(self, t, d):
        self.copies.wait_recv(self.y_slot[t, d], self.buf.at[0], self.along[d])
        self.send(self.c_slot[t, d], t, d, self.other)

    def end(self):
        for t in (0, 1):
            for d in (0, 1, 2, 3):
                self.copies.wait_recv(self.c_slot[t, d], self.buf.at[0], self.other)


def project_kernel(
    rows_ref, weight_ref, kv_ref, turned_ref, rows_all, weight_all, send_sem, recv_sem
):
    sec, seq, mp = place()
    copies = Copies(send_sem, recv_sem)
    mp_peer = {d: (sec, seq, lax.rem(mp + d, 4)) for d in (1, 2, 3)}
    sec_peer = {d: (lax.rem(sec + d, 4), seq, mp) for d in (1, 2, 3)}
    across, other, along = seq_peers(sec, seq, mp)
    own = sec * 4 + mp
    diagonal = seq == own
    mirror = (seq // 4, own, lax.rem(seq, 4))

    barrier = pltpu.get_barrier_semaphore()
    peers = (
        [mp_peer[d] for d in (1, 2, 3)]
        + [sec_peer[d] for d in (1, 2, 3)]
        + [along[d] for d in (1, 2, 3)]
        + [across, other]
    )
    for peer in peers:
        pl.semaphore_signal(barrier, inc=1, device_id=peer, device_id_type=MESH)

    @pl.when(jnp.logical_not(diagonal))
    def _():
        pl.semaphore_signal(barrier, inc=1, device_id=mirror, device_id_type=MESH)

    rows_all[own] = rows_ref[...]
    weight_all[seq] = weight_ref[0]
    pl.semaphore_wait(barrier, len(peers) + 1 - diagonal.astype(jnp.int32))

    gather_w = SeqGather(copies, weight_all, sec, seq, mp)
    gather_kv = SeqGather(copies, kv_ref, sec, seq, mp)
    m_slot = {d: copies.slot() for d in (1, 2, 3)}
    x_slot = {(e, d): copies.slot() for e in (0, 1, 2, 3) for d in (1, 2, 3)}
    turn_slot = copies.slot()

    def pass_on(e):
        block = rows_all.at[sec * 4 + lax.rem(mp + 4 - e, 4)]
        if e:
            copies.wait_recv(m_slot[e], block, mp_peer[e])
        for d in (1, 3, 2):
            copies.start(x_slot[e, d], block, block, sec_peer[d])

    block = rows_all.at[own]
    for d in (1, 3):
        copies.start(m_slot[d], block, block, mp_peer[d])
    pass_on(0)
    gather_w.begin_near()
    pass_on(1)
    gather_w.begin_far()
    pass_on(3)
    copies.start(m_slot[2], block, block, mp_peer[2])
    for d in (1, 3, 2):
        gather_w.relay_core(0, d)
    gather_w.relay_across()
    pass_on(2)
    for d in (1, 3, 2):
        gather_w.relay_core(1, d)
    for e in (0, 1, 3, 2):
        for d in (1, 3, 2):
            copies.wait_recv(x_slot[e, d], rows_all.at[0], sec_peer[d])

    turn = copies.make(turn_slot, rows_all.at[own], turned_ref, mirror)

    @pl.when(diagonal)
    def _():
        turned_ref[...] = rows_ref[...]

    @pl.when(jnp.logical_not(diagonal))
    def _():
        turn.start()

    gather_w.end()

    def term(f, total):
        return total + jnp.dot(
            rows_all[f], weight_all[f], preferred_element_type=jnp.float32
        )

    total = lax.fori_loop(0, 16, term, jnp.zeros(kv_ref.shape[1:], jnp.float32))
    kv_ref[seq] = total.astype(kv_ref.dtype)

    gather_kv.begin_far()
    gather_kv.begin_near()
    for d in (1, 3, 2):
        gather_kv.relay_core(0, d)
    gather_kv.relay_across()
    for d in (1, 3, 2):
        gather_kv.relay_core(1, d)
    gather_kv.end()

    @pl.when(jnp.logical_not(diagonal))
    def _():
        turn.wait()

    copies.finish()


def project(rows, weight):
    tok, feat = rows.shape
    cols = weight.shape[2]
    sems = 46
    vmem = pl.BlockSpec(memory_space=pltpu.VMEM)
    return pl.pallas_call(
        project_kernel,
        out_shape=(
            jax.ShapeDtypeStruct((16, tok, cols), jnp.bfloat16),
            jax.ShapeDtypeStruct((tok, feat), jnp.bfloat16),
        ),
        in_specs=[vmem, vmem],
        out_specs=(vmem, vmem),
        scratch_shapes=[
            pltpu.VMEM((16, tok, feat), jnp.bfloat16),
            pltpu.VMEM((16, feat, cols), jnp.bfloat16),
            pltpu.SemaphoreType.DMA((sems,)),
            pltpu.SemaphoreType.DMA((sems,)),
        ],
        compiler_params=pltpu.CompilerParams(
            collective_id=0, has_side_effects=True, vmem_limit_bytes=VMEM_LIMIT
        ),
        name="project",
    )(rows, weight)


def attention_kernel(
    order,
    q_ref,
    g_ref,
    kv_ref,
    rows_ref,
    att_ref,
    dq_ref,
    out_ref,
    q_all,
    g_all,
    kv_t,
    score,
    prob,
    dscore,
    dquery,
    stats,
    rows_t,
    acc,
    keep,
    core_out,
    core_in,
    y_out,
    y_in,
    z_out,
    z_in,
    grad,
    send_sem,
    recv_sem,
):
    sec, seq, mp = place()
    copies = Copies(send_sem, recv_sem)
    yy = seq // 4
    core = lax.rem(seq, 2)
    across, other, along = seq_peers(sec, seq, mp)
    sec_peer = {d: (lax.rem(sec + d, 4), seq, mp) for d in (1, 2, 3)}
    mp_peer = {d: (sec, seq, lax.rem(mp + d, 4)) for d in (1, 2, 3)}
    greet(
        [mp_peer[d] for d in (1, 2, 3)]
        + [sec_peer[d] for d in (1, 2, 3)]
        + [along[d] for d in (1, 2, 3)]
        + [across, other]
    )

    m_slot = {d: copies.slot() for d in (1, 2, 3)}
    x_slot = {(e, d): copies.slot() for e in range(4) for d in (1, 2, 3)}
    core_slot = [copies.slot() for _ in range(4)]
    y_slot = {d: copies.slot() for d in (1, 2, 3)}
    z_slot = [copies.slot() for _ in range(PIECES)]
    ag_slot = {(p, d): copies.slot() for p in range(PIECES) for d in (1, 2, 3)}
    cg_slot = {(p, d): copies.slot() for p in range(PIECES) for d in (0, 1, 2, 3)}

    tok = q_ref.shape[0]
    half = tok // SLOTS
    group = q_ref.shape[1] // HD
    lanes = group * half
    part_rows = 4 * tok
    scale = HD ** (-0.5)
    rate = scale * LOG2E

    def token_block(t):
        return rows_t.at[t // 2, pl.ds(pl.multiple_of(lax.rem(t, 2) * tok, 16), tok), :]

    def pass_on(e):
        block = token_block(sec * 4 + lax.rem(mp + 4 - e, 4))
        if e:
            copies.wait_recv(m_slot[e], block, mp_peer[e])
        for d in (1, 3, 2):
            copies.start(x_slot[e, d], block, block, sec_peer[d])

    token_block(sec * 4 + mp)[...] = rows_ref[...]
    for d in (1, 3, 2):
        block = token_block(sec * 4 + mp)
        copies.start(m_slot[d], block, block, mp_peer[d])
    pass_on(0)

    def lane(i):
        return slice(i * lanes, (i + 1) * lanes)

    for i in range(SLOTS):
        for h in range(group):
            at = i * lanes + h * half
            rows = slice(i * half, (i + 1) * half)
            q_all[at : at + half, :] = q_ref[rows, h * HD : (h + 1) * HD]
            g_all[at : at + half, :] = g_ref[rows, h * HD : (h + 1) * HD]
    for j in range(4):
        kv_t[j] = kv_ref[j * part_rows : (j + 1) * part_rows, :].T

    for i in range(SLOTS):
        skew = lax.broadcasted_iota(jnp.int32, (half, lanes), 0) - lax.rem(
            lax.broadcasted_iota(jnp.int32, (half, lanes), 1), half
        )
        here = order[seq * SLOTS + i]
        peak = jnp.full((8, lanes), -1e30, jnp.float32)
        for j in range(4):
            raw = contract(
                kv_ref[j * part_rows : (j + 1) * part_rows, :HD], q_all[lane(i), :], 1, 1
            )
            for b in range(part_rows // half):
                ahead = (here - order[j * (part_rows // half) + b]) * half
                seen = jnp.where(skew <= ahead, raw[b * half : (b + 1) * half, :], -1e30)
                at = j * part_rows + b * half
                score[at : at + half, lane(i)] = seen
                peak = jnp.maximum(peak, jnp.max(seen.reshape(half // 8, 8, lanes), axis=0))
        peak = jnp.max(peak, axis=0, keepdims=True)
        total = jnp.zeros((8, lanes), jnp.float32)
        for j in range(4):
            at = slice(j * part_rows, (j + 1) * part_rows)
            expo = jnp.exp2((score[at, lane(i)] - peak) * rate)
            score[at, lane(i)] = expo
            total += jnp.sum(expo.reshape(part_rows // 8, 8, lanes), axis=0)
        part = 1.0 / jnp.sum(total, axis=0, keepdims=True)
        out = jnp.zeros((HD, lanes), jnp.float32)
        for j in range(4):
            at = slice(j * part_rows, (j + 1) * part_rows)
            weights = (score[at, lane(i)] * part).astype(jnp.bfloat16)
            prob[at, lane(i)] = weights
            out += jnp.dot(kv_t[j, HD:], weights, preferred_element_type=jnp.float32)
        out = out.astype(jnp.bfloat16).astype(jnp.float32)
        delta = jnp.sum(g_all[lane(i), :].astype(jnp.float32).T * out, axis=0, keepdims=True)
        stats[0, :, lane(i)] = jnp.broadcast_to(delta, (8, lanes))
        stats[1, :, lane(i)] = jnp.broadcast_to(part * scale, (8, lanes))
        out = out.T.astype(jnp.bfloat16)
        for h in range(group):
            att_ref[i * half : (i + 1) * half, h * HD : (h + 1) * HD] = out[
                h * half : (h + 1) * half, :
            ]
        if i == 1:
            pass_on(1)
        if i == 2:
            pass_on(3)

    def back(d):
        yt = lax.rem(yy + d, 4)
        rows = pl.ds(pl.multiple_of(yt * part_rows, 16), part_rows)
        for i in range(SLOTS):
            dprob = contract(kv_ref[rows, HD:], g_all[lane(i), :], 1, 1)
            dscore[:, lane(i)] = (
                score[rows, lane(i)]
                * stats[1, :1, lane(i)]
                * (dprob - stats[0, :1, lane(i)])
            ).astype(jnp.bfloat16)
        dkey = jnp.dot(dscore[...], q_all[...], preferred_element_type=jnp.float32)
        dvalue = jnp.dot(prob[rows, :], g_all[...], preferred_element_type=jnp.float32)
        acc[..., :HD] = dkey.reshape(2, 2, tok, HD)
        acc[..., HD:] = dvalue.reshape(2, 2, tok, HD)
        core_out[d] = acc[:, 1 - core].astype(jnp.bfloat16)
        copies.start(core_slot[d], core_out.at[d], core_in.at[d], other)
        keep[d] = acc[:, core]
        more = jnp.dot(kv_t[yt, :HD], dscore[...], preferred_element_type=jnp.float32)
        if d == 2:
            dquery[...] = more
        else:
            dquery[...] += more

    def send_along(d):
        copies.wait_recv(core_slot[d], core_in.at[d], other)
        y_out[d - 1] = (keep[d] + core_in[d].astype(jnp.float32)).astype(jnp.bfloat16)
        copies.start(y_slot[d], y_out.at[d - 1], y_in.at[d - 1], along[d])

    back(2)
    back(1)
    send_along(2)
    pass_on(2)
    back(3)
    send_along(1)
    back(0)
    send_along(3)
    for i in range(SLOTS):
        turned = dquery[:, lane(i)].T.astype(jnp.bfloat16)
        for h in range(group):
            dq_ref[i * half : (i + 1) * half, h * HD : (h + 1) * HD] = turned[
                h * half : (h + 1) * half, :
            ]
    copies.wait_recv(core_slot[0], core_in.at[0], other)
    for d in (1, 3, 2):
        copies.wait_recv(y_slot[d], y_in.at[d - 1], along[d])

    piece = tok // PIECES

    def piece_rows(p):
        return slice(p * piece, (p + 1) * piece)

    for p in range(PIECES):
        rows = piece_rows(p)
        total = keep[0, :, rows] + core_in[0, :, rows].astype(jnp.float32)
        for d in (1, 2, 3):
            total += y_in[d - 1, :, rows].astype(jnp.float32)
        z_out[p] = total.astype(jnp.bfloat16)
        copies.start(z_slot[p], z_out.at[p], z_in.at[p], across)
    for p in range(PIECES):
        copies.wait_recv(z_slot[p], z_in.at[p], across)
        grad[yy, :, core, piece_rows(p)] = (
            z_out[p].astype(jnp.float32) + z_in[p].astype(jnp.float32)
        ).astype(jnp.bfloat16)
        own = grad.at[yy, :, core, piece_rows(p)]
        for d in (1, 3, 2):
            copies.start(ag_slot[p, d], own, own, along[d])
        copies.start(cg_slot[p, 0], own, own, other)
    for p in range(PIECES):
        for d in (1, 3, 2):
            block = grad.at[lax.rem(yy + 4 - d, 4), :, core, piece_rows(p)]
            copies.wait_recv(ag_slot[p, d], block, along[d])
            copies.start(cg_slot[p, d], block, block, other)
    for j in range(4):
        for d in (1, 3, 2):
            copies.wait_recv(x_slot[j, d], token_block(0), sec_peer[d])
    for p in range(PIECES):
        for d in (0, 1, 3, 2):
            copies.wait_recv(cg_slot[p, d], grad.at[0, :, 0, piece_rows(p)], other)

    result = jnp.zeros(out_ref.shape, jnp.float32)
    for k in range(8):
        block = grad[k // 2, k % 2].reshape(2 * tok, 2 * HD)
        result += contract(rows_t[k], block, 0, 0)
    out_ref[...] = result

    copies.finish()


def attention(order, queries, out_grad, kv, rows):
    tok, cols = queries.shape
    feat = rows.shape[1]
    keys = kv.shape[0]
    lanes = cols // HD * tok
    sems = 3 + 12 + 4 + 3 + PIECES * 8
    vmem = pl.BlockSpec(memory_space=pltpu.VMEM)
    half = (2, tok, 2 * HD)
    pieces = (PIECES, 2, tok // PIECES, 2 * HD)
    return pl.pallas_call(
        attention_kernel,
        out_shape=(
            jax.ShapeDtypeStruct((tok, cols), jnp.bfloat16),
            jax.ShapeDtypeStruct((tok, cols), jnp.bfloat16),
            jax.ShapeDtypeStruct((feat, 2 * HD), jnp.float32),
        ),
        in_specs=[pl.BlockSpec(memory_space=pltpu.SMEM), vmem, vmem, vmem, vmem],
        out_specs=(vmem, vmem, vmem),
        scratch_shapes=[
            pltpu.VMEM((lanes, HD), jnp.bfloat16),
            pltpu.VMEM((lanes, HD), jnp.bfloat16),
            pltpu.VMEM((4, 2 * HD, keys // 4), jnp.bfloat16),
            pltpu.VMEM((keys, lanes), jnp.float32),
            pltpu.VMEM((keys, lanes), jnp.bfloat16),
            pltpu.VMEM((keys // 4, lanes), jnp.bfloat16),
            pltpu.VMEM((HD, lanes), jnp.float32),
            pltpu.VMEM((2, 8, lanes), jnp.float32),
            pltpu.VMEM((8, 2 * tok, feat), jnp.bfloat16),
            pltpu.VMEM((2,) + half, jnp.float32),
            pltpu.VMEM((4,) + half, jnp.float32),
            pltpu.VMEM((4,) + half, jnp.bfloat16),
            pltpu.VMEM((4,) + half, jnp.bfloat16),
            pltpu.VMEM((3,) + half, jnp.bfloat16),
            pltpu.VMEM((3,) + half, jnp.bfloat16),
            pltpu.VMEM(pieces, jnp.bfloat16),
            pltpu.VMEM(pieces, jnp.bfloat16),
            pltpu.VMEM((4, 2) + half, jnp.bfloat16),
            pltpu.SemaphoreType.DMA((sems,)),
            pltpu.SemaphoreType.DMA((sems,)),
        ],
        compiler_params=pltpu.CompilerParams(
            collective_id=1, has_side_effects=True, vmem_limit_bytes=VMEM_LIMIT
        ),
        name="attention",
    )(order, queries, out_grad, kv, rows)


def body(rows40, queries, kv_weight, out_grad, block_order):
    tok = rows40.shape[0]
    kv, turned = project(rows40, kv_weight)
    attended, query_grad, grad = attention(
        block_order, queries[0], out_grad[0], kv.reshape(16 * tok, 2 * HD), turned
    )
    return (attended[None], query_grad[None], grad[None])


def solution(mesh):
    return jax.shard_map(
        body,
        mesh=mesh,
        in_specs=(
            P("seq", ("section", "mp")),
            P("section", "seq", "mp"),
            P("section", "seq", "mp"),
            P("section", "seq", "mp"),
            P(),
        ),
        out_specs=(P("section", "seq", "mp"), P("section", "seq", "mp"), P("section", "seq", "mp")),
        check_vma=False,
    )
```

time: 208 us -> 147 us (0.71)
  the two profiles are of different devices: /device:TPU:97 before, /device:TPU:1 now
where the time goes in v2:
time: 147 us; the launch traced here: 146 us
  Pallas kernels  141 us (96%)
  local copies, waits for them, and re-layouts  4.39 us (3%)
    pallas_call x1, Pallas kernels, project(): pl.pallas_call(project_kernel, out_shape=(jax.ShapeDtypeStruct((16, tok,...  78.5 us
    pallas_call x1, Pallas kernels, attention(): pl.pallas_call(attention_kernel, out_shape=(jax.ShapeDtypeStruct((tok, co...  62.8 us
    unnamed x5, local copies, waits for them, and re-layouts  4.39 us

profile of v2, /device:TPU:1, one launch (start us, length us, event | category | flops | bytes accessed | tf_op | source)
XLA Modules:
  0.0 146.4 jit_solution(17926635836775694666)
XLA Ops:
  0.6 78.5 %project.1 = (bf16[16,192,256]{2,1,0:T(8,128)(2,1)}, bf16[192,512]{1,0:T(8,128)(2,1)}) custom-call(bf16[192,512]{1,0:T(8,128)(2,1)} %rows_ref.1, bf16[1,512,256]{2,1,0:T(8,128)(2,1)} %weight_ref.1), custom_call_target="tpu_custom_call" | custom-call | tf_op jit(solution)/shard_map/project/pallas_call | solution.py:231
  79.1 62.8 %attention.1 = (bf16[192,1024]{1,0:T(8,128)(2,1)}, bf16[192,1024]{1,0:T(8,128)(2,1)}, f32[512,256]{1,0:T(8,128)}) custom-call(s32[64]{0:T(128)} %order.1, bf16[192,1024]{1,0:T(8,128)(2,1)} %bitcast.10, bf16[192,1024]{1,0:T(8,128)(2,1)} %bitcast.11, bf16[3072,256]{1,0:T(8,128)(2,1)} %bitcast.6, bf16[192,512]{1,0:T(8,128)(2,1)} %get-tuple-element.9.rows_ref), custom_call_target="tpu_custom_call" | custom-call | tf_op jit(solution)/shard_map/attention/pallas_call | solution.py:481
  142.0 0.0 copy-start
  142.0 1.8 %copy.11 = bf16[1,192,1024]{2,1,0:T(8,128)(2,1)} copy(bf16[1,192,1024]{2,1,0:T(8,128)(2,1)} %bitcast.9) | data formatting | bytes 786432
  143.8 1.8 %copy.12 = bf16[1,192,1024]{2,1,0:T(8,128)(2,1)} copy(bf16[1,192,1024]{2,1,0:T(8,128)(2,1)} %bitcast.8) | data formatting | bytes 786432
  145.6 0.0 copy-done
  145.6 0.8 copy.13
Async XLA Ops:
  142.0 3.6 %copy-start = (f32[512,256]{1,0:T(8,128)S(1)}, f32[512,256]{1,0:T(8,128)}, u32[]{:S(2)}) copy-start(f32[512,256]{1,0:T(8,128)} %get-tuple-element.12) | copy-start | bytes 1572868

commit v3 on v2

--- a/solution.py
+++ b/solution.py
@@ -125,139 +125,18 @@
                 self.copies.wait_recv(self.c_slot[t, d], self.buf.at[0], self.other)
 
 
-def project_kernel(
-    rows_ref, weight_ref, kv_ref, turned_ref, rows_all, weight_all, send_sem, recv_sem
-):
-    sec, seq, mp = place()
-    copies = Copies(send_sem, recv_sem)
-    mp_peer = {d: (sec, seq, lax.rem(mp + d, 4)) for d in (1, 2, 3)}
-    sec_peer = {d: (lax.rem(sec + d, 4), seq, mp) for d in (1, 2, 3)}
-    across, other, along = seq_peers(sec, seq, mp)
-    own = sec * 4 + mp
-    diagonal = seq == own
-    mirror = (seq // 4, own, lax.rem(seq, 4))
-
-    barrier = pltpu.get_barrier_semaphore()
-    peers = (
-        [mp_peer[d] for d in (1, 2, 3)]
-        + [sec_peer[d] for d in (1, 2, 3)]
-        + [along[d] for d in (1, 2, 3)]
-        + [across, other]
-    )
-    for peer in peers:
-        pl.semaphore_signal(barrier, inc=1, device_id=peer, device_id_type=MESH)
-
-    @pl.when(jnp.logical_not(diagonal))
-    def _():
-        pl.semaphore_signal(barrier, inc=1, device_id=mirror, device_id_type=MESH)
-
-    rows_all[own] = rows_ref[...]
-    weight_all[seq] = weight_ref[0]
-    pl.semaphore_wait(barrier, len(peers) + 1 - diagonal.astype(jnp.int32))
-
-    gather_w = SeqGather(copies, weight_all, sec, seq, mp)
-    gather_kv = SeqGather(copies, kv_ref, sec, seq, mp)
-    m_slot = {d: copies.slot() for d in (1, 2, 3)}
-    x_slot = {(e, d): copies.slot() for e in (0, 1, 2, 3) for d in (1, 2, 3)}
-    turn_slot = copies.slot()
-
-    def pass_on(e):
-        block = rows_all.at[sec * 4 + lax.rem(mp + 4 - e, 4)]
-        if e:
-            copies.wait_recv(m_slot[e], block, mp_peer[e])
-        for d in (1, 3, 2):
-            copies.start(x_slot[e, d], block, block, sec_peer[d])
-
-    block = rows_all.at[own]
-    for d in (1, 3):
-        copies.start(m_slot[d], block, block, mp_peer[d])
-    pass_on(0)
-    gather_w.begin_near()
-    pass_on(1)
-    gather_w.begin_far()
-    pass_on(3)
-    copies.start(m_slot[2], block, block, mp_peer[2])
-    for d in (1, 3, 2):
-        gather_w.relay_core(0, d)
-    gather_w.relay_across()
-    pass_on(2)
-    for d in (1, 3, 2):
-        gather_w.relay_core(1, d)
-    for e in (0, 1, 3, 2):
-        for d in (1, 3, 2):
-            copies.wait_recv(x_slot[e, d], rows_all.at[0], sec_peer[d])
-
-    turn = copies.make(turn_slot, rows_all.at[own], turned_ref, mirror)
-
-    @pl.when(diagonal)
-    def _():
-        turned_ref[...] = rows_ref[...]
-
-    @pl.when(jnp.logical_not(diagonal))
-    def _():
-        turn.start()
-
-    gather_w.end()
-
-    def term(f, total):
-        return total + jnp.dot(
-            rows_all[f], weight_all[f], preferred_element_type=jnp.float32
-        )
-
-    total = lax.fori_loop(0, 16, term, jnp.zeros(kv_ref.shape[1:], jnp.float32))
-    kv_ref[seq] = total.astype(kv_ref.dtype)
-
-    gather_kv.begin_far()
-    gather_kv.begin_near()
-    for d in (1, 3, 2):
-        gather_kv.relay_core(0, d)
-    gather_kv.relay_across()
-    for d in (1, 3, 2):
-        gather_kv.relay_core(1, d)
-    gather_kv.end()
-
-    @pl.when(jnp.logical_not(diagonal))
-    def _():
-        turn.wait()
-
-    copies.finish()
-
-
-def project(rows, weight):
-    tok, feat = rows.shape
-    cols = weight.shape[2]
-    sems = 46
-    vmem = pl.BlockSpec(memory_space=pltpu.VMEM)
-    return pl.pallas_call(
-        project_kernel,
-        out_shape=(
-            jax.ShapeDtypeStruct((16, tok, cols), jnp.bfloat16),
-            jax.ShapeDtypeStruct((tok, feat), jnp.bfloat16),
-        ),
-        in_specs=[vmem, vmem],
-        out_specs=(vmem, vmem),
-        scratch_shapes=[
-            pltpu.VMEM((16, tok, feat), jnp.bfloat16),
-            pltpu.VMEM((16, feat, cols), jnp.bfloat16),
-            pltpu.SemaphoreType.DMA((sems,)),
-            pltpu.SemaphoreType.DMA((sems,)),
-        ],
-        compiler_params=pltpu.CompilerParams(
-            collective_id=0, has_side_effects=True, vmem_limit_bytes=VMEM_LIMIT
-        ),
-        name="project",
-    )(rows, weight)
-
-
-def attention_kernel(
+def layer_kernel(
     order,
     q_ref,
     g_ref,
-    kv_ref,
     rows_ref,
+    weight_ref,
     att_ref,
     dq_ref,
     out_ref,
+    rows_all,
+    weight_all,
+    kv_all,
     q_all,
     g_all,
     kv_t,
@@ -286,13 +165,33 @@
     across, other, along = seq_peers(sec, seq, mp)
     sec_peer = {d: (lax.rem(sec + d, 4), seq, mp) for d in (1, 2, 3)}
     mp_peer = {d: (sec, seq, lax.rem(mp + d, 4)) for d in (1, 2, 3)}
-    greet(
+    own = sec * 4 + mp
+    diagonal = seq == own
+    mirror = (seq // 4, own, lax.rem(seq, 4))
+
+    barrier = pltpu.get_barrier_semaphore()
+    peers = (
         [mp_peer[d] for d in (1, 2, 3)]
         + [sec_peer[d] for d in (1, 2, 3)]
         + [along[d] for d in (1, 2, 3)]
         + [across, other]
     )
-
+    for peer in peers:
+        pl.semaphore_signal(barrier, inc=1, device_id=peer, device_id_type=MESH)
+
+    @pl.when(jnp.logical_not(diagonal))
+    def _():
+        pl.semaphore_signal(barrier, inc=1, device_id=mirror, device_id_type=MESH)
+
+    rows_all[own] = rows_ref[...]
+    weight_all[seq] = weight_ref[0]
+    pl.semaphore_wait(barrier, len(peers) + 1 - diagonal.astype(jnp.int32))
+
+    gather_w = SeqGather(copies, weight_all, sec, seq, mp)
+    gather_kv = SeqGather(copies, kv_all, sec, seq, mp)
+    rows_slot = {d: copies.slot() for d in (1, 2, 3)}
+    along_x = {(e, d): copies.slot() for e in range(4) for d in (1, 2, 3)}
+    turn_slot = copies.slot()
     m_slot = {d: copies.slot() for d in (1, 2, 3)}
     x_slot = {(e, d): copies.slot() for e in range(4) for d in (1, 2, 3)}
     core_slot = [copies.slot() for _ in range(4)]
@@ -319,54 +218,131 @@
         for d in (1, 3, 2):
             copies.start(x_slot[e, d], block, block, sec_peer[d])
 
-    token_block(sec * 4 + mp)[...] = rows_ref[...]
-    for d in (1, 3, 2):
-        block = token_block(sec * 4 + mp)
-        copies.start(m_slot[d], block, block, mp_peer[d])
-    pass_on(0)
-
     def lane(i):
         return slice(i * lanes, (i + 1) * lanes)
 
+    def pass_rows(e):
+        block = rows_all.at[sec * 4 + lax.rem(mp + 4 - e, 4)]
+        if e:
+            copies.wait_recv(rows_slot[e], block, mp_peer[e])
+        for d in (1, 3, 2):
+            copies.start(along_x[e, d], block, block, sec_peer[d])
+
+    block = rows_all.at[own]
+    for d in (1, 3):
+        copies.start(rows_slot[d], block, block, mp_peer[d])
+    pass_rows(0)
+    gather_w.begin_near()
     for i in range(SLOTS):
         for h in range(group):
             at = i * lanes + h * half
             rows = slice(i * half, (i + 1) * half)
             q_all[at : at + half, :] = q_ref[rows, h * HD : (h + 1) * HD]
             g_all[at : at + half, :] = g_ref[rows, h * HD : (h + 1) * HD]
-    for j in range(4):
-        kv_t[j] = kv_ref[j * part_rows : (j + 1) * part_rows, :].T
-
+    pass_rows(1)
+    gather_w.begin_far()
+    pass_rows(3)
+    copies.start(rows_slot[2], block, block, mp_peer[2])
+    for d in (1, 3, 2):
+        gather_w.relay_core(0, d)
+    gather_w.relay_across()
+    pass_rows(2)
+    for d in (1, 3, 2):
+        gather_w.relay_core(1, d)
+    for e in (0, 1, 3, 2):
+        for d in (1, 3, 2):
+            copies.wait_recv(along_x[e, d], block, sec_peer[d])
+
+    turn = copies.make(turn_slot, block, token_block(seq), mirror)
+
+    @pl.when(diagonal)
+    def _():
+        token_block(own)[...] = rows_ref[...]
+
+    @pl.when(jnp.logical_not(diagonal))
+    def _():
+        turn.start()
+
+    gather_w.end()
+
+    def term(f, total):
+        return total + jnp.dot(
+            rows_all[f], weight_all[f], preferred_element_type=jnp.float32
+        )
+
+    total = lax.fori_loop(0, 16, term, jnp.zeros((tok, 2 * HD), jnp.float32))
+    kv_all[seq] = total.astype(jnp.bfloat16)
+
+    gather_kv.begin_far()
+    gather_kv.begin_near()
+
+    def keys_of(d):
+        first = lax.rem(yy + 4 - d, 4) * 4
+        return kv_all[pl.ds(first, 4)].reshape(part_rows, 2 * HD)
+
+    skew = lax.broadcasted_iota(jnp.int32, (half, lanes), 0) - lax.rem(
+        lax.broadcasted_iota(jnp.int32, (half, lanes), 1), half
+    )
+    peaks = [jnp.full((8, lanes), -1e30, jnp.float32) for _ in range(SLOTS)]
+
+    def look(d):
+        for t in (0, 1):
+            copies.wait_recv(gather_kv.c_slot[t, d], kv_all.at[0], other)
+        part_kv = keys_of(d)
+        kv_t[d] = part_kv.T
+        first = lax.rem(yy + 4 - d, 4) * (part_rows // half)
+        for i in range(SLOTS):
+            raw = contract(part_kv[:, :HD], q_all[lane(i), :], 1, 1)
+            for b in range(part_rows // half):
+                ahead = (order[seq * SLOTS + i] - order[first + b]) * half
+                seen = jnp.where(skew <= ahead, raw[b * half : (b + 1) * half, :], -1e30)
+                at = d * part_rows + b * half
+                score[at : at + half, lane(i)] = seen
+                peaks[i] = jnp.maximum(
+                    peaks[i], jnp.max(seen.reshape(half // 8, 8, lanes), axis=0)
+                )
+
+    for d in (1, 3, 2):
+        gather_kv.relay_core(0, d)
+    gather_kv.relay_across()
+
+    def pass_on(e):
+        block = token_block(sec * 4 + lax.rem(mp + 4 - e, 4))
+        if e:
+            copies.wait_recv(m_slot[e], block, mp_peer[e])
+        for d in (1, 3, 2):
+            copies.start(x_slot[e, d], block, block, sec_peer[d])
+
+    look(0)
+    for d in (1, 3, 2):
+        gather_kv.relay_core(1, d)
+
+    @pl.when(jnp.logical_not(diagonal))
+    def _():
+        turn.wait_send()
+        copies.wait_recv(turn_slot, token_block(own), mirror)
+
+    for d in (1, 3, 2):
+        copies.start(m_slot[d], token_block(own), token_block(own), mp_peer[d])
+    pass_on(0)
+    look(1)
+    look(3)
+    look(2)
     for i in range(SLOTS):
-        skew = lax.broadcasted_iota(jnp.int32, (half, lanes), 0) - lax.rem(
-            lax.broadcasted_iota(jnp.int32, (half, lanes), 1), half
-        )
-        here = order[seq * SLOTS + i]
-        peak = jnp.full((8, lanes), -1e30, jnp.float32)
-        for j in range(4):
-            raw = contract(
-                kv_ref[j * part_rows : (j + 1) * part_rows, :HD], q_all[lane(i), :], 1, 1
-            )
-            for b in range(part_rows // half):
-                ahead = (here - order[j * (part_rows // half) + b]) * half
-                seen = jnp.where(skew <= ahead, raw[b * half : (b + 1) * half, :], -1e30)
-                at = j * part_rows + b * half
-                score[at : at + half, lane(i)] = seen
-                peak = jnp.maximum(peak, jnp.max(seen.reshape(half // 8, 8, lanes), axis=0))
-        peak = jnp.max(peak, axis=0, keepdims=True)
+        peak = jnp.max(peaks[i], axis=0, keepdims=True)
         total = jnp.zeros((8, lanes), jnp.float32)
-        for j in range(4):
-            at = slice(j * part_rows, (j + 1) * part_rows)
+        for d in range(4):
+            at = slice(d * part_rows, (d + 1) * part_rows)
             expo = jnp.exp2((score[at, lane(i)] - peak) * rate)
             score[at, lane(i)] = expo
             total += jnp.sum(expo.reshape(part_rows // 8, 8, lanes), axis=0)
         part = 1.0 / jnp.sum(total, axis=0, keepdims=True)
         out = jnp.zeros((HD, lanes), jnp.float32)
-        for j in range(4):
-            at = slice(j * part_rows, (j + 1) * part_rows)
+        for d in range(4):
+            at = slice(d * part_rows, (d + 1) * part_rows)
             weights = (score[at, lane(i)] * part).astype(jnp.bfloat16)
             prob[at, lane(i)] = weights
-            out += jnp.dot(kv_t[j, HD:], weights, preferred_element_type=jnp.float32)
+            out += jnp.dot(kv_t[d, HD:], weights, preferred_element_type=jnp.float32)
         out = out.astype(jnp.bfloat16).astype(jnp.float32)
         delta = jnp.sum(g_all[lane(i), :].astype(jnp.float32).T * out, axis=0, keepdims=True)
         stats[0, :, lane(i)] = jnp.broadcast_to(delta, (8, lanes))
@@ -376,16 +352,19 @@
             att_ref[i * half : (i + 1) * half, h * HD : (h + 1) * HD] = out[
                 h * half : (h + 1) * half, :
             ]
+        if i == 0:
+            pass_on(1)
         if i == 1:
-            pass_on(1)
-        if i == 2:
             pass_on(3)
+        if i == 3:
+            pass_on(2)
 
     def back(d):
-        yt = lax.rem(yy + d, 4)
-        rows = pl.ds(pl.multiple_of(yt * part_rows, 16), part_rows)
+        part = (4 - d) % 4
+        rows = slice(part * part_rows, (part + 1) * part_rows)
+        values = keys_of(part)[:, HD:]
         for i in range(SLOTS):
-            dprob = contract(kv_ref[rows, HD:], g_all[lane(i), :], 1, 1)
+            dprob = contract(values, g_all[lane(i), :], 1, 1)
             dscore[:, lane(i)] = (
                 score[rows, lane(i)]
                 * stats[1, :1, lane(i)]
@@ -398,7 +377,7 @@
         core_out[d] = acc[:, 1 - core].astype(jnp.bfloat16)
         copies.start(core_slot[d], core_out.at[d], core_in.at[d], other)
         keep[d] = acc[:, core]
-        more = jnp.dot(kv_t[yt, :HD], dscore[...], preferred_element_type=jnp.float32)
+        more = jnp.dot(kv_t[part, :HD], dscore[...], preferred_element_type=jnp.float32)
         if d == 2:
             dquery[...] = more
         else:
@@ -412,7 +391,6 @@
     back(2)
     back(1)
     send_along(2)
-    pass_on(2)
     back(3)
     send_along(1)
     back(0)
@@ -444,10 +422,10 @@
         grad[yy, :, core, piece_rows(p)] = (
             z_out[p].astype(jnp.float32) + z_in[p].astype(jnp.float32)
         ).astype(jnp.bfloat16)
-        own = grad.at[yy, :, core, piece_rows(p)]
-        for d in (1, 3, 2):
-            copies.start(ag_slot[p, d], own, own, along[d])
-        copies.start(cg_slot[p, 0], own, own, other)
+        mine = grad.at[yy, :, core, piece_rows(p)]
+        for d in (1, 3, 2):
+            copies.start(ag_slot[p, d], mine, mine, along[d])
+        copies.start(cg_slot[p, 0], mine, mine, other)
     for p in range(PIECES):
         for d in (1, 3, 2):
             block = grad.at[lax.rem(yy + 4 - d, 4), :, core, piece_rows(p)]
@@ -455,7 +433,7 @@
             copies.start(cg_slot[p, d], block, block, other)
     for j in range(4):
         for d in (1, 3, 2):
-            copies.wait_recv(x_slot[j, d], token_block(0), sec_peer[d])
+            copies.wait_recv(x_slot[j, d], token_block(own), sec_peer[d])
     for p in range(PIECES):
         for d in (0, 1, 3, 2):
             copies.wait_recv(cg_slot[p, d], grad.at[0, :, 0, piece_rows(p)], other)
@@ -469,25 +447,28 @@
     copies.finish()
 
 
-def attention(order, queries, out_grad, kv, rows):
+def layer(order, queries, out_grad, rows, weight):
     tok, cols = queries.shape
     feat = rows.shape[1]
-    keys = kv.shape[0]
+    keys = 16 * tok
     lanes = cols // HD * tok
-    sems = 3 + 12 + 4 + 3 + PIECES * 8
+    sems = 15 + 15 + 15 + 1 + 15 + 4 + 3 + PIECES * 8
     vmem = pl.BlockSpec(memory_space=pltpu.VMEM)
     half = (2, tok, 2 * HD)
     pieces = (PIECES, 2, tok // PIECES, 2 * HD)
     return pl.pallas_call(
-        attention_kernel,
+        layer_kernel,
         out_shape=(
             jax.ShapeDtypeStruct((tok, cols), jnp.bfloat16),
             jax.ShapeDtypeStruct((tok, cols), jnp.bfloat16),
             jax.ShapeDtypeStruct((feat, 2 * HD), jnp.float32),
         ),
-        in_specs=[pl.BlockSpec(memory_space=pltpu.SMEM), vmem, vmem, vmem, vmem],
+        in_specs=[pl.BlockSpec(memory_space=pltpu.SMEM)] + [vmem] * 4,
         out_specs=(vmem, vmem, vmem),
         scratch_shapes=[
+            pltpu.VMEM((16, tok, feat), jnp.bfloat16),
+            pltpu.VMEM((16, feat, 2 * HD), jnp.bfloat16),
+            pltpu.VMEM((16, tok, 2 * HD), jnp.bfloat16),
             pltpu.VMEM((lanes, HD), jnp.bfloat16),
             pltpu.VMEM((lanes, HD), jnp.bfloat16),
             pltpu.VMEM((4, 2 * HD, keys // 4), jnp.bfloat16),
@@ -510,18 +491,14 @@
             pltpu.SemaphoreType.DMA((sems,)),
         ],
         compiler_params=pltpu.CompilerParams(
-            collective_id=1, has_side_effects=True, vmem_limit_bytes=VMEM_LIMIT
+            collective_id=0, has_side_effects=True, vmem_limit_bytes=VMEM_LIMIT
         ),
-        name="attention",
-    )(order, queries, out_grad, kv, rows)
+        name="layer",
+    )(order, queries, out_grad, rows, weight)
 
 
 def body(rows40, queries, kv_weight, out_grad, block_order):
-    tok = rows40.shape[0]
-    kv, turned = project(rows40, kv_weight)
-    attended, query_grad, grad = attention(
-        block_order, queries[0], out_grad[0], kv.reshape(16 * tok, 2 * HD), turned
-    )
+    attended, query_grad, grad = layer(block_order, queries[0], out_grad[0], rows40, kv_weight)
     return (attended[None], query_grad[None], grad[None])
 
 

time: 147 us -> 138 us (0.939)
  the two profiles are of different devices: /device:TPU:1 before, /device:TPU:33 now
where the time goes in v3:
time: 138 us; the launch traced here: 137 us
  Pallas kernels  133 us (96%)
  local copies, waits for them, and re-layouts  3.8 us (3%)
    pallas_call x1, Pallas kernels, layer(): pl.pallas_call(layer_kernel, out_shape=(jax.ShapeDtypeStruct((tok, cols),...  133 us
    unnamed x7, local copies, waits for them, and re-layouts  3.8 us

profile of v3, /device:TPU:33, one launch (start us, length us, event | category | flops | bytes accessed | tf_op | source)
XLA Modules:
  0.0 137.4 jit_solution(15349991397759016939)
XLA Ops:
  0.6 133.0 %layer.1 = (bf16[192,1024]{1,0:T(8,128)(2,1)}, bf16[192,1024]{1,0:T(8,128)(2,1)}, f32[512,256]{1,0:T(8,128)}) custom-call(s32[64]{0:T(128)} %order.1, bf16[192,1024]{1,0:T(8,128)(2,1)} %bitcast.8, bf16[192,1024]{1,0:T(8,128)(2,1)} %bitcast.9, bf16[192,512]{1,0:T(8,128)(2,1)} %rows_ref.1, bf16[1,512,256]{2,1,0:T(8,128)(2,1)} %weight_ref.1), custom_call_target="tpu_custom_call" | custom-call | tf_op jit(solution)/shard_map/layer/pallas_call | solution.py:459
  133.6 0.0 copy-start.1
  133.6 1.8 %copy.11 = bf16[1,192,1024]{2,1,0:T(8,128)(2,1)} copy(bf16[1,192,1024]{2,1,0:T(8,128)(2,1)} %bitcast.7) | data formatting | bytes 786432
  135.5 0.0 copy-done.1
  135.5 0.0 copy-start
  135.5 0.7 copy.12
  136.2 0.4 copy-done
  136.6 0.8 copy.13
Async XLA Ops:
  133.6 1.8 %copy-start.1 = (bf16[192,1024]{1,0:T(8,128)(2,1)S(1)}, bf16[192,1024]{1,0:T(8,128)(2,1)}, u32[]{:S(2)}) copy-start(bf16[192,1024]{1,0:T(8,128)(2,1)} %get-tuple-element.7) | copy-start | bytes 1179652
  135.5 1.2 copy-start

commit v4 on v3

--- a/solution.py
+++ b/solution.py
@@ -30,6 +30,7 @@
         self.recv_sem = recv_sem
         self.count = 0
         self.started = []
+        self.guarded = []
 
     def slot(self):
         self.count += 1
@@ -53,9 +54,21 @@
     def wait_recv(self, slot, buf, device):
         self.make(slot, buf, buf, device).wait_recv()
 
+    def start_if(self, slot, ref, device, condition):
+        @pl.when(condition())
+        def _():
+            self.make(slot, ref(), ref(), device).start()
+
+        self.guarded.append((slot, ref, device, condition))
+
     def finish(self):
         for copy in self.started:
             copy.wait_send()
+        for slot, ref, device, condition in self.guarded:
+
+            @pl.when(condition())
+            def _():
+                self.make(slot, ref(), ref(), device).wait_send()
 
 
 def place():
@@ -82,47 +95,46 @@
 
 
 class SeqGather:
-    def __init__(self, copies, buf, sec, seq, mp):
+    def __init__(self, copies, buf, rows, sec, seq, mp):
         self.copies = copies
         self.buf = buf
+        self.rows = rows
         self.seq = seq
         self.across, self.other, self.along = seq_peers(sec, seq, mp)
         self.z_slot = copies.slot()
         self.y_slot = {(t, d): copies.slot() for t in (0, 1) for d in (1, 2, 3)}
         self.c_slot = {(t, d): copies.slot() for t in (0, 1) for d in (0, 1, 2, 3)}
 
-    def index(self, t, d):
-        own = lax.rem(self.seq + 16 - 4 * d, 16)
-        if t == 0:
-            return own
-        return own + 2 - 4 * lax.rem(own // 2, 2)
+    def block(self, t, d):
+        owner = lax.rem(self.seq + 16 - 4 * d, 16)
+        if t:
+            owner = owner + 2 - 4 * lax.rem(owner // 2, 2)
+        return self.buf.at[owner, self.rows]
 
     def send(self, slot, t, d, device):
-        block = self.buf.at[self.index(t, d)]
+        block = self.block(t, d)
         self.copies.start(slot, block, block, device)
 
     def begin_far(self):
         self.send(self.z_slot, 0, 0, self.across)
 
-    def begin_near(self):
-        for d in (1, 3, 2):
-            self.send(self.y_slot[0, d], 0, 0, self.along[d])
-        self.send(self.c_slot[0, 0], 0, 0, self.other)
+    def begin_near(self, t=0):
+        for d in (1, 3, 2):
+            self.send(self.y_slot[t, d], t, 0, self.along[d])
+        self.send(self.c_slot[t, 0], t, 0, self.other)
 
     def relay_across(self):
-        self.copies.wait_recv(self.z_slot, self.buf.at[0], self.across)
-        for d in (1, 3, 2):
-            self.send(self.y_slot[1, d], 1, 0, self.along[d])
-        self.send(self.c_slot[1, 0], 1, 0, self.other)
-
-    def relay_core(self, t, d):
-        self.copies.wait_recv(self.y_slot[t, d], self.buf.at[0], self.along[d])
-        self.send(self.c_slot[t, d], t, d, self.other)
-
-    def end(self):
+        self.copies.wait_recv(self.z_slot, self.block(1, 0), self.across)
+        self.begin_near(1)
+
+    def relay_core(self, t):
+        for d in (1, 3, 2):
+            self.copies.wait_recv(self.y_slot[t, d], self.block(t, d), self.along[d])
+            self.send(self.c_slot[t, d], t, d, self.other)
+
+    def end(self, d):
         for t in (0, 1):
-            for d in (0, 1, 2, 3):
-                self.copies.wait_recv(self.c_slot[t, d], self.buf.at[0], self.other)
+            self.copies.wait_recv(self.c_slot[t, d], self.block(t, d), self.other)
 
 
 def layer_kernel(
@@ -146,6 +158,7 @@
     dquery,
     stats,
     rows_t,
+    rows_tt,
     acc,
     keep,
     core_out,
@@ -166,34 +179,45 @@
     sec_peer = {d: (lax.rem(sec + d, 4), seq, mp) for d in (1, 2, 3)}
     mp_peer = {d: (sec, seq, lax.rem(mp + d, 4)) for d in (1, 2, 3)}
     own = sec * 4 + mp
-    diagonal = seq == own
+    zhi = lax.rem(seq // 2, 2)
+    turning = mp // 2 != zhi
     mirror = (seq // 4, own, lax.rem(seq, 4))
+    aslant = {d: (sec, lax.rem(seq + 4 * d, 16) + 1 - 2 * core, mp) for d in (1, 2, 3)}
 
     barrier = pltpu.get_barrier_semaphore()
     peers = (
         [mp_peer[d] for d in (1, 2, 3)]
         + [sec_peer[d] for d in (1, 2, 3)]
         + [along[d] for d in (1, 2, 3)]
+        + [aslant[d] for d in (1, 2, 3)]
         + [across, other]
     )
     for peer in peers:
         pl.semaphore_signal(barrier, inc=1, device_id=peer, device_id_type=MESH)
 
-    @pl.when(jnp.logical_not(diagonal))
+    @pl.when(turning)
     def _():
         pl.semaphore_signal(barrier, inc=1, device_id=mirror, device_id_type=MESH)
 
     rows_all[own] = rows_ref[...]
     weight_all[seq] = weight_ref[0]
-    pl.semaphore_wait(barrier, len(peers) + 1 - diagonal.astype(jnp.int32))
-
-    gather_w = SeqGather(copies, weight_all, sec, seq, mp)
-    gather_kv = SeqGather(copies, kv_all, sec, seq, mp)
-    rows_slot = {d: copies.slot() for d in (1, 2, 3)}
-    along_x = {(e, d): copies.slot() for e in range(4) for d in (1, 2, 3)}
+    pl.semaphore_wait(barrier, len(peers) + turning.astype(jnp.int32))
+
+    w_rows, kv_rows = weight_all.shape[1] // 2, kv_all.shape[1] // 2
+    gather_w = [
+        SeqGather(copies, weight_all, pl.ds(p * w_rows, w_rows), sec, seq, mp) for p in (0, 1)
+    ]
+    gather_kv = [
+        SeqGather(copies, kv_all, pl.ds(p * kv_rows, kv_rows), sec, seq, mp) for p in (0, 1)
+    ]
+    sides = [(side, hops) for hops in (1, 2, 3) for side in (-1, 1)]
+    line_slot = {key: copies.slot() for key in sides}
+    along_x = {(key, d): copies.slot() for key in [(0, 0)] + sides for d in (1, 2, 3)}
     turn_slot = copies.slot()
-    m_slot = {d: copies.slot() for d in (1, 2, 3)}
-    x_slot = {(e, d): copies.slot() for e in range(4) for d in (1, 2, 3)}
+    m_slot = {(j, d): copies.slot() for j in (0, 1) for d in (1, 2, 3)}
+    x_slot = {(j, d): copies.slot() for j in (0, 1) for d in (1, 2, 3)}
+    y_same = {d: copies.slot() for d in (1, 2, 3)}
+    y_cross = {d: copies.slot() for d in (0, 1, 2, 3)}
     core_slot = [copies.slot() for _ in range(4)]
     y_slot = {d: copies.slot() for d in (1, 2, 3)}
     z_slot = [copies.slot() for _ in range(PIECES)]
@@ -221,60 +245,96 @@
     def lane(i):
         return slice(i * lanes, (i + 1) * lanes)
 
-    def pass_rows(e):
-        block = rows_all.at[sec * 4 + lax.rem(mp + 4 - e, 4)]
-        if e:
-            copies.wait_recv(rows_slot[e], block, mp_peer[e])
-        for d in (1, 3, 2):
-            copies.start(along_x[e, d], block, block, sec_peer[d])
-
-    block = rows_all.at[own]
-    for d in (1, 3):
-        copies.start(rows_slot[d], block, block, mp_peer[d])
-    pass_rows(0)
-    gather_w.begin_near()
+    below = (sec, seq, jnp.maximum(mp - 1, 0))
+    above = (sec, seq, jnp.minimum(mp + 1, 3))
+
+    def there(key):
+        side, hops = key
+        return mp >= hops if side < 0 else mp + hops <= 3
+
+    def rows_of(key):
+        side, hops = key
+        return rows_all.at[sec * 4 + mp + side * hops]
+
+    def spread(key):
+        for d in (1, 3, 2):
+            copies.start_if(
+                along_x[key, d],
+                lambda: rows_of(key),
+                sec_peer[d],
+                lambda: there(key),
+            )
+
+    def from_line(hops):
+        for side in (-1, 1):
+            key = (side, hops)
+
+            @pl.when(there(key))
+            def _():
+                copies.wait_recv(line_slot[key], rows_of(key), below if side < 0 else above)
+
+            if hops < 3:
+                to_line(key)
+            spread(key)
+
+    def to_line(key):
+        side, hops = key
+        copies.start_if(
+            line_slot[side, hops + 1],
+            lambda: rows_of(key),
+            above if side < 0 else below,
+            lambda: jnp.logical_and(there(key), mp < 3 if side < 0 else mp > 0),
+        )
+
+    to_line((-1, 0))
+    to_line((1, 0))
+    spread((0, 0))
+    gather_w[0].begin_far()
+    gather_w[0].begin_near()
+    gather_w[1].begin_near()
     for i in range(SLOTS):
         for h in range(group):
             at = i * lanes + h * half
             rows = slice(i * half, (i + 1) * half)
             q_all[at : at + half, :] = q_ref[rows, h * HD : (h + 1) * HD]
             g_all[at : at + half, :] = g_ref[rows, h * HD : (h + 1) * HD]
-    pass_rows(1)
-    gather_w.begin_far()
-    pass_rows(3)
-    copies.start(rows_slot[2], block, block, mp_peer[2])
-    for d in (1, 3, 2):
-        gather_w.relay_core(0, d)
-    gather_w.relay_across()
-    pass_rows(2)
-    for d in (1, 3, 2):
-        gather_w.relay_core(1, d)
-    for e in (0, 1, 3, 2):
-        for d in (1, 3, 2):
-            copies.wait_recv(along_x[e, d], block, sec_peer[d])
-
-    turn = copies.make(turn_slot, block, token_block(seq), mirror)
-
-    @pl.when(diagonal)
-    def _():
-        token_block(own)[...] = rows_ref[...]
-
-    @pl.when(jnp.logical_not(diagonal))
+    from_line(1)
+    gather_w[1].begin_far()
+    gather_w[0].relay_across()
+    from_line(2)
+    gather_w[0].relay_core(0)
+    gather_w[1].relay_core(0)
+    gather_w[1].relay_across()
+    turn = copies.make(turn_slot, rows_all.at[own], token_block(seq), mirror)
+
+    @pl.when(turning)
     def _():
         turn.start()
 
-    gather_w.end()
-
-    def term(f, total):
-        return total + jnp.dot(
-            rows_all[f], weight_all[f], preferred_element_type=jnp.float32
-        )
-
-    total = lax.fori_loop(0, 16, term, jnp.zeros((tok, 2 * HD), jnp.float32))
+    from_line(3)
+    gather_w[0].relay_core(1)
+    gather_w[1].relay_core(1)
+
+    for key in [(0, 0)] + sides:
+
+        @pl.when(there(key))
+        def _():
+            for d in (1, 3, 2):
+                copies.wait_recv(along_x[key, d], rows_of(key), sec_peer[d])
+
+    for p in (0, 1):
+        for d in range(4):
+            gather_w[p].end(d)
+
+    total = jnp.zeros((tok, 2 * HD), jnp.float32)
+    for f in range(16):
+        total += jnp.dot(rows_all[f], weight_all[f], preferred_element_type=jnp.float32)
     kv_all[seq] = total.astype(jnp.bfloat16)
 
-    gather_kv.begin_far()
-    gather_kv.begin_near()
+    for p in (0, 1):
+        gather_kv[p].begin_far()
+    for p in (0, 1):
+        gather_kv[p].begin_near()
 
     def keys_of(d):
         first = lax.rem(yy + 4 - d, 4) * 4
@@ -286,8 +346,8 @@
     peaks = [jnp.full((8, lanes), -1e30, jnp.float32) for _ in range(SLOTS)]
 
     def look(d):
-        for t in (0, 1):
-            copies.wait_recv(gather_kv.c_slot[t, d], kv_all.at[0], other)
+        for p in (0, 1):
+            gather_kv[p].end(d)
         part_kv = keys_of(d)
         kv_t[d] = part_kv.T
         first = lax.rem(yy + 4 - d, 4) * (part_rows // half)
@@ -302,29 +362,63 @@
                     peaks[i], jnp.max(seen.reshape(half // 8, 8, lanes), axis=0)
                 )
 
-    for d in (1, 3, 2):
-        gather_kv.relay_core(0, d)
-    gather_kv.relay_across()
-
-    def pass_on(e):
-        block = token_block(sec * 4 + lax.rem(mp + 4 - e, 4))
-        if e:
-            copies.wait_recv(m_slot[e], block, mp_peer[e])
-        for d in (1, 3, 2):
-            copies.start(x_slot[e, d], block, block, sec_peer[d])
-
+    first_far = 2 - 2 * zhi
+
+    def far_block(j):
+        return token_block(sec * 4 + first_far + j)
+
+    def has_far(j):
+        return jnp.logical_and(turning, lax.rem(mp, 2) == j)
+
+    def begin_line():
+        @pl.when(turning)
+        def _():
+            turn.wait_send()
+            copies.wait_recv(turn_slot, token_block(own), mirror)
+
+        for j in (0, 1):
+            for d in (1, 3, 2):
+                copies.start_if(
+                    m_slot[j, d], lambda j=j: far_block(j), mp_peer[d], lambda j=j: has_far(j)
+                )
+
+    def pass_on(j):
+        for d in (1, 2, 3):
+            @pl.when(first_far + j == lax.rem(mp + 4 - d, 4))
+            def _():
+                copies.wait_recv(m_slot[j, d], far_block(j), mp_peer[d])
+
+        for d in (1, 3, 2):
+            copies.start(x_slot[j, d], far_block(j), far_block(j), sec_peer[d])
+
+    def along_y():
+        token_block(seq)[...] = rows_all[seq]
+        for d in (1, 3, 2):
+            aim = lax.rem(seq + 4 * d, 16)
+            copies.start(y_same[d], rows_all.at[aim], token_block(seq), along[d])
+            aim = aim + 1 - 2 * core
+            copies.start(y_cross[d], rows_all.at[aim], token_block(seq), aslant[d])
+        copies.start(y_cross[0], rows_all.at[seq + 1 - 2 * core], token_block(seq), other)
+
+    def end_blocks():
+        for d in (1, 3, 2):
+            copies.wait_recv(y_same[d], token_block(seq), along[d])
+            copies.wait_recv(y_cross[d], token_block(seq), aslant[d])
+        copies.wait_recv(y_cross[0], token_block(seq), other)
+        for j in (0, 1):
+            for d in (1, 3, 2):
+                copies.wait_recv(x_slot[j, d], far_block(j), sec_peer[d])
+
+    gather_kv[0].relay_core(0)
+    gather_kv[0].relay_across()
+    gather_kv[1].relay_core(0)
+    gather_kv[1].relay_across()
+
+    begin_line()
     look(0)
-    for d in (1, 3, 2):
-        gather_kv.relay_core(1, d)
-
-    @pl.when(jnp.logical_not(diagonal))
-    def _():
-        turn.wait_send()
-        copies.wait_recv(turn_slot, token_block(own), mirror)
-
-    for d in (1, 3, 2):
-        copies.start(m_slot[d], token_block(own), token_block(own), mp_peer[d])
-    pass_on(0)
+    gather_kv[0].relay_core(1)
+    gather_kv[1].relay_core(1)
+    along_y()
     look(1)
     look(3)
     look(2)
@@ -352,14 +446,10 @@
             att_ref[i * half : (i + 1) * half, h * HD : (h + 1) * HD] = out[
                 h * half : (h + 1) * half, :
             ]
-        if i == 0:
-            pass_on(1)
-        if i == 1:
-            pass_on(3)
-        if i == 3:
-            pass_on(2)
-
-    def back(d):
+        if i < 2:
+            pass_on(i)
+
+    def back(d, between=None):
         part = (4 - d) % 4
         rows = slice(part * part_rows, (part + 1) * part_rows)
         values = keys_of(part)[:, HD:]
@@ -370,6 +460,8 @@
                 * stats[1, :1, lane(i)]
                 * (dprob - stats[0, :1, lane(i)])
             ).astype(jnp.bfloat16)
+        if between:
+            send_along(between)
         dkey = jnp.dot(dscore[...], q_all[...], preferred_element_type=jnp.float32)
         dvalue = jnp.dot(prob[rows, :], g_all[...], preferred_element_type=jnp.float32)
         acc[..., :HD] = dkey.reshape(2, 2, tok, HD)
@@ -389,12 +481,9 @@
         copies.start(y_slot[d], y_out.at[d - 1], y_in.at[d - 1], along[d])
 
     back(2)
-    back(1)
-    send_along(2)
-    back(3)
-    send_along(1)
-    back(0)
-    send_along(3)
+    back(1, between=2)
+    back(3, between=1)
+    back(0, between=3)
     for i in range(SLOTS):
         turned = dquery[:, lane(i)].T.astype(jnp.bfloat16)
         for h in range(group):
@@ -417,6 +506,9 @@
             total += y_in[d - 1, :, rows].astype(jnp.float32)
         z_out[p] = total.astype(jnp.bfloat16)
         copies.start(z_slot[p], z_out.at[p], z_in.at[p], across)
+    end_blocks()
+    for k in range(8):
+        rows_tt[k] = rows_t[k].T
     for p in range(PIECES):
         copies.wait_recv(z_slot[p], z_in.at[p], across)
         grad[yy, :, core, piece_rows(p)] = (
@@ -431,18 +523,22 @@
             block = grad.at[lax.rem(yy + 4 - d, 4), :, core, piece_rows(p)]
             copies.wait_recv(ag_slot[p, d], block, along[d])
             copies.start(cg_slot[p, d], block, block, other)
-    for j in range(4):
-        for d in (1, 3, 2):
-            copies.wait_recv(x_slot[j, d], token_block(own), sec_peer[d])
-    for p in range(PIECES):
-        for d in (0, 1, 3, 2):
+    for d in (0, 1, 3, 2):
+        for p in range(PIECES):
             copies.wait_recv(cg_slot[p, d], grad.at[0, :, 0, piece_rows(p)], other)
-
-    result = jnp.zeros(out_ref.shape, jnp.float32)
-    for k in range(8):
-        block = grad[k // 2, k % 2].reshape(2 * tok, 2 * HD)
-        result += contract(rows_t[k], block, 0, 0)
-    out_ref[...] = result
+        yt = lax.rem(yy + 4 - d, 4)
+        more = sum(
+            jnp.dot(
+                rows_tt[2 * yt + t],
+                grad[yt, t].reshape(2 * tok, 2 * HD),
+                preferred_element_type=jnp.float32,
+            )
+            for t in (0, 1)
+        )
+        if d == 0:
+            out_ref[...] = more
+        else:
+            out_ref[...] += more
 
     copies.finish()
 
@@ -452,7 +548,7 @@
     feat = rows.shape[1]
     keys = 16 * tok
     lanes = cols // HD * tok
-    sems = 15 + 15 + 15 + 1 + 15 + 4 + 3 + PIECES * 8
+    sems = 4 * 15 + 6 + 21 + 1 + 19 + 4 + 3 + PIECES * 8
     vmem = pl.BlockSpec(memory_space=pltpu.VMEM)
     half = (2, tok, 2 * HD)
     pieces = (PIECES, 2, tok // PIECES, 2 * HD)
@@ -478,6 +574,7 @@
             pltpu.VMEM((HD, lanes), jnp.float32),
             pltpu.VMEM((2, 8, lanes), jnp.float32),
             pltpu.VMEM((8, 2 * tok, feat), jnp.bfloat16),
+            pltpu.VMEM((8, feat, 2 * tok), jnp.bfloat16),
             pltpu.VMEM((2,) + half, jnp.float32),
             pltpu.VMEM((4,) + half, jnp.float32),
             pltpu.VMEM((4,) + half, jnp.bfloat16),

time: 138 us -> 128 us (0.928)
  the two profiles are of different devices: /device:TPU:33 before, /device:TPU:1 now
where the time goes in v4:
time: 128 us; the launch traced here: 125 us
  Pallas kernels  121 us (95%)
  local copies, waits for them, and re-layouts  3.8 us (3%)
    pallas_call x1, Pallas kernels, layer(): pl.pallas_call(layer_kernel, out_shape=(jax.ShapeDtypeStruct((tok, cols),...  121 us
    unnamed x7, local copies, waits for them, and re-layouts  3.8 us

profile of v4, /device:TPU:1, one launch (start us, length us, event | category | flops | bytes accessed | tf_op | source)
XLA Modules:
  0.0 125.2 jit_solution(1916568018510858706)
XLA Ops:
  0.6 120.7 %layer.1 = (bf16[192,1024]{1,0:T(8,128)(2,1)}, bf16[192,1024]{1,0:T(8,128)(2,1)}, f32[512,256]{1,0:T(8,128)}) custom-call(s32[64]{0:T(128)} %order.1, bf16[192,1024]{1,0:T(8,128)(2,1)} %bitcast.8, bf16[192,1024]{1,0:T(8,128)(2,1)} %bitcast.9, bf16[192,512]{1,0:T(8,128)(2,1)} %rows_ref.1, bf16[1,512,256]{2,1,0:T(8,128)(2,1)} %weight_ref.1), custom_call_target="tpu_custom_call" | custom-call | tf_op jit(solution)/shard_map/layer/pallas_call | solution.py:555
  121.4 0.0 copy-start.1
  121.4 1.8 %copy.11 = bf16[1,192,1024]{2,1,0:T(8,128)(2,1)} copy(bf16[1,192,1024]{2,1,0:T(8,128)(2,1)} %bitcast.7) | data formatting | bytes 786432
  123.2 0.0 copy-done.1
  123.2 0.0 copy-start
  123.2 0.7 copy.12
  124.0 0.4 copy-done
  124.4 0.8 copy.13
Async XLA Ops:
  121.4 1.8 %copy-start.1 = (bf16[192,1024]{1,0:T(8,128)(2,1)S(1)}, bf16[192,1024]{1,0:T(8,128)(2,1)}, u32[]{:S(2)}) copy-start(bf16[192,1024]{1,0:T(8,128)(2,1)} %get-tuple-element.7) | copy-start | bytes 1179652
  123.2 1.2 copy-start

commit v5 on v4

--- a/solution.py
+++ b/solution.py
@@ -132,9 +132,8 @@
             self.copies.wait_recv(self.y_slot[t, d], self.block(t, d), self.along[d])
             self.send(self.c_slot[t, d], t, d, self.other)
 
-    def end(self, d):
-        for t in (0, 1):
-            self.copies.wait_recv(self.c_slot[t, d], self.block(t, d), self.other)
+    def end(self, d, t):
+        self.copies.wait_recv(self.c_slot[t, d], self.block(t, d), self.other)
 
 
 def layer_kernel(
@@ -315,53 +314,6 @@
     gather_w[0].relay_core(1)
     gather_w[1].relay_core(1)
 
-    for key in [(0, 0)] + sides:
-
-        @pl.when(there(key))
-        def _():
-            for d in (1, 3, 2):
-                copies.wait_recv(along_x[key, d], rows_of(key), sec_peer[d])
-
-    for p in (0, 1):
-        for d in range(4):
-            gather_w[p].end(d)
-
-    total = jnp.zeros((tok, 2 * HD), jnp.float32)
-    for f in range(16):
-        total += jnp.dot(rows_all[f], weight_all[f], preferred_element_type=jnp.float32)
-    kv_all[seq] = total.astype(jnp.bfloat16)
-
-    for p in (0, 1):
-        gather_kv[p].begin_far()
-    for p in (0, 1):
-        gather_kv[p].begin_near()
-
-    def keys_of(d):
-        first = lax.rem(yy + 4 - d, 4) * 4
-        return kv_all[pl.ds(first, 4)].reshape(part_rows, 2 * HD)
-
-    skew = lax.broadcasted_iota(jnp.int32, (half, lanes), 0) - lax.rem(
-        lax.broadcasted_iota(jnp.int32, (half, lanes), 1), half
-    )
-    peaks = [jnp.full((8, lanes), -1e30, jnp.float32) for _ in range(SLOTS)]
-
-    def look(d):
-        for p in (0, 1):
-            gather_kv[p].end(d)
-        part_kv = keys_of(d)
-        kv_t[d] = part_kv.T
-        first = lax.rem(yy + 4 - d, 4) * (part_rows // half)
-        for i in range(SLOTS):
-            raw = contract(part_kv[:, :HD], q_all[lane(i), :], 1, 1)
-            for b in range(part_rows // half):
-                ahead = (order[seq * SLOTS + i] - order[first + b]) * half
-                seen = jnp.where(skew <= ahead, raw[b * half : (b + 1) * half, :], -1e30)
-                at = d * part_rows + b * half
-                score[at : at + half, lane(i)] = seen
-                peaks[i] = jnp.maximum(
-                    peaks[i], jnp.max(seen.reshape(half // 8, 8, lanes), axis=0)
-                )
-
     first_far = 2 - 2 * zhi
 
     def far_block(j):
@@ -390,6 +342,60 @@
 
         for d in (1, 3, 2):
             copies.start(x_slot[j, d], far_block(j), far_block(j), sec_peer[d])
+
+    begin_line()
+    for key in [(0, 0)] + sides:
+
+        @pl.when(there(key))
+        def _():
+            for d in (1, 3, 2):
+                copies.wait_recv(along_x[key, d], rows_of(key), sec_peer[d])
+
+    for p in (0, 1):
+        for d in range(4):
+            gather_w[p].end(d, 0)
+            gather_w[p].end(d, 1)
+
+    total = jnp.zeros((tok, 2 * HD), jnp.float32)
+    for f in range(16):
+        total += jnp.dot(rows_all[f], weight_all[f], preferred_element_type=jnp.float32)
+    kv_all[seq] = total.astype(jnp.bfloat16)
+
+    for p in (0, 1):
+        gather_kv[p].begin_far()
+    for p in (0, 1):
+        gather_kv[p].begin_near()
+
+    side_rows = 2 * tok
+
+    def side_first(d, t):
+        return lax.rem(yy + 4 - d, 4) * 4 + 2 * (zhi if t == 0 else 1 - zhi)
+
+    def keys_of(d, t):
+        return kv_all[pl.ds(side_first(d, t), 2)].reshape(side_rows, 2 * HD)
+
+    skew = lax.broadcasted_iota(jnp.int32, (half, lanes), 0) - lax.rem(
+        lax.broadcasted_iota(jnp.int32, (half, lanes), 1), half
+    )
+    peaks = [jnp.full((8, lanes), -1e30, jnp.float32) for _ in range(SLOTS)]
+
+    def look(d, t):
+        for p in (0, 1):
+            gather_kv[p].end(d, t)
+        side_kv = keys_of(d, t)
+        start = d * part_rows + t * side_rows
+        kv_t[d, :, t * side_rows : (t + 1) * side_rows] = side_kv.T
+        first = side_first(d, t) * SLOTS
+        for i in range(SLOTS):
+            raw = contract(side_kv[:, :HD], q_all[lane(i), :], 1, 1)
+            for b in range(side_rows // half):
+                ahead = (order[seq * SLOTS + i] - order[first + b]) * half
+                seen = jnp.where(skew <= ahead, raw[b * half : (b + 1) * half, :], -1e30)
+                at = start + b * half
+                score[at : at + half, lane(i)] = seen
+                peaks[i] = jnp.maximum(
+                    peaks[i], jnp.max(seen.reshape(half // 8, 8, lanes), axis=0)
+                )
 
     def along_y():
         token_block(seq)[...] = rows_all[seq]
@@ -410,18 +416,21 @@
                 copies.wait_recv(x_slot[j, d], far_block(j), sec_peer[d])
 
     gather_kv[0].relay_core(0)
+    pass_on(0)
+    pass_on(1)
     gather_kv[0].relay_across()
     gather_kv[1].relay_core(0)
     gather_kv[1].relay_across()
 
-    begin_line()
-    look(0)
+    look(0, 0)
+    look(1, 0)
     gather_kv[0].relay_core(1)
+    look(3, 0)
     gather_kv[1].relay_core(1)
     along_y()
-    look(1)
-    look(3)
-    look(2)
+    look(2, 0)
+    for d in (0, 1, 3, 2):
+        look(d, 1)
     for i in range(SLOTS):
         peak = jnp.max(peaks[i], axis=0, keepdims=True)
         total = jnp.zeros((8, lanes), jnp.float32)
@@ -446,13 +455,11 @@
             att_ref[i * half : (i + 1) * half, h * HD : (h + 1) * HD] = out[
                 h * half : (h + 1) * half, :
             ]
-        if i < 2:
-            pass_on(i)
 
     def back(d, between=None):
         part = (4 - d) % 4
         rows = slice(part * part_rows, (part + 1) * part_rows)
-        values = keys_of(part)[:, HD:]
+        values = jnp.concatenate([keys_of(part, t)[:, HD:] for t in (0, 1)], axis=0)
         for i in range(SLOTS):
             dprob = contract(values, g_all[lane(i), :], 1, 1)
             dscore[:, lane(i)] = (
@@ -464,8 +471,10 @@
             send_along(between)
         dkey = jnp.dot(dscore[...], q_all[...], preferred_element_type=jnp.float32)
         dvalue = jnp.dot(prob[rows, :], g_all[...], preferred_element_type=jnp.float32)
-        acc[..., :HD] = dkey.reshape(2, 2, tok, HD)
-        acc[..., HD:] = dvalue.reshape(2, 2, tok, HD)
+        for t, side in ((0, zhi), (1, 1 - zhi)):
+            rows_here = slice(t * side_rows, (t + 1) * side_rows)
+            acc[side, :, :, :HD] = dkey[rows_here].reshape(2, tok, HD)
+            acc[side, :, :, HD:] = dvalue[rows_here].reshape(2, tok, HD)
         core_out[d] = acc[:, 1 - core].astype(jnp.bfloat16)
         copies.start(core_slot[d], core_out.at[d], core_in.at[d], other)
         keep[d] = acc[:, core]

time: 128 us -> 127 us (level); the launches traced: 125 us -> 127 us
    pallas_call x1, Pallas kernels: 121 us -> 122 us  [layer(): pl.pallas_call(layer_kernel, out_shape=(jax.ShapeDtypeStruct((tok, cols),...]
where the time goes in v5:
time: 127 us
  Pallas kernels  122 us (96%)
  local copies, waits for them, and re-layouts  3.8 us (3%)
    pallas_call x1, Pallas kernels, layer(): pl.pallas_call(layer_kernel, out_shape=(jax.ShapeDtypeStruct((tok, cols),...  122 us
    unnamed x7, local copies, waits for them, and re-layouts  3.8 us

profile of v5, /device:TPU:1, one launch (start us, length us, event | category | flops | bytes accessed | tf_op | source)
XLA Modules:
  0.0 126.7 jit_solution(12894492914702993096)
XLA Ops:
  0.6 122.2 %layer.1 = (bf16[192,1024]{1,0:T(8,128)(2,1)}, bf16[192,1024]{1,0:T(8,128)(2,1)}, f32[512,256]{1,0:T(8,128)}) custom-call(s32[64]{0:T(128)} %order.1, bf16[192,1024]{1,0:T(8,128)(2,1)} %bitcast.8, bf16[192,1024]{1,0:T(8,128)(2,1)} %bitcast.9, bf16[192,512]{1,0:T(8,128)(2,1)} %rows_ref.1, bf16[1,512,256]{2,1,0:T(8,128)(2,1)} %weight_ref.1), custom_call_target="tpu_custom_call" | custom-call | tf_op jit(solution)/shard_map/layer/pallas_call | solution.py:564
  122.9 0.0 copy-start.1
  122.9 1.8 %copy.11 = bf16[1,192,1024]{2,1,0:T(8,128)(2,1)} copy(bf16[1,192,1024]{2,1,0:T(8,128)(2,1)} %bitcast.7) | data formatting | bytes 786432
  124.7 0.0 copy-done.1
  124.7 0.0 copy-start
  124.7 0.7 copy.12
  125.4 0.4 copy-done
  125.9 0.8 copy.13
Async XLA Ops:
  122.9 1.8 %copy-start.1 = (bf16[192,1024]{1,0:T(8,128)(2,1)S(1)}, bf16[192,1024]{1,0:T(8,128)(2,1)}, u32[]{:S(2)}) copy-start(bf16[192,1024]{1,0:T(8,128)(2,1)} %get-tuple-element.7) | copy-start | bytes 1179652
  124.7 1.2 copy-start

commit v6 on v5

--- a/solution.py
+++ b/solution.py
@@ -344,21 +344,25 @@
             copies.start(x_slot[j, d], far_block(j), far_block(j), sec_peer[d])
 
     begin_line()
+    for p in (0, 1):
+        for d in range(4):
+            gather_w[p].end(d, 0)
+            gather_w[p].end(d, 1)
+
+    keep[0, 0] = jnp.zeros((tok, 2 * HD), jnp.float32)
     for key in [(0, 0)] + sides:
 
         @pl.when(there(key))
         def _():
             for d in (1, 3, 2):
                 copies.wait_recv(along_x[key, d], rows_of(key), sec_peer[d])
-
-    for p in (0, 1):
-        for d in range(4):
-            gather_w[p].end(d, 0)
-            gather_w[p].end(d, 1)
-
-    total = jnp.zeros((tok, 2 * HD), jnp.float32)
-    for f in range(16):
-        total += jnp.dot(rows_all[f], weight_all[f], preferred_element_type=jnp.float32)
+            more = jnp.zeros((tok, 2 * HD), jnp.float32)
+            for d in range(4):
+                f = lax.rem(sec + d, 4) * 4 + mp + key[0] * key[1]
+                more += jnp.dot(rows_all[f], weight_all[f], preferred_element_type=jnp.float32)
+            keep[0, 0] += more
+
+    total = keep[0, 0]
     kv_all[seq] = total.astype(jnp.bfloat16)
 
     for p in (0, 1):

time: 127 us -> 127 us (level)
  no operation moved by 1% of the time
where the time goes in v6:
time: 127 us; the launch traced here: 126 us
  Pallas kernels  122 us (96%)
  local copies, waits for them, and re-layouts  3.8 us (3%)
    pallas_call x1, Pallas kernels, layer(): pl.pallas_call(layer_kernel, out_shape=(jax.ShapeDtypeStruct((tok, cols),...  122 us
    unnamed x7, local copies, waits for them, and re-layouts  3.8 us

profile of v6, /device:TPU:1, one launch (start us, length us, event | category | flops | bytes accessed | tf_op | source)
XLA Modules:
  0.0 126.1 jit_solution(15747046055247598420)
XLA Ops:
  0.6 121.7 %layer.1 = (bf16[192,1024]{1,0:T(8,128)(2,1)}, bf16[192,1024]{1,0:T(8,128)(2,1)}, f32[512,256]{1,0:T(8,128)}) custom-call(s32[64]{0:T(128)} %order.1, bf16[192,1024]{1,0:T(8,128)(2,1)} %bitcast.8, bf16[192,1024]{1,0:T(8,128)(2,1)} %bitcast.9, bf16[192,512]{1,0:T(8,128)(2,1)} %rows_ref.1, bf16[1,512,256]{2,1,0:T(8,128)(2,1)} %weight_ref.1), custom_call_target="tpu_custom_call" | custom-call | tf_op jit(solution)/shard_map/layer/pallas_call | solution.py:568
  122.3 0.0 copy-start.1
  122.3 1.8 %copy.11 = bf16[1,192,1024]{2,1,0:T(8,128)(2,1)} copy(bf16[1,192,1024]{2,1,0:T(8,128)(2,1)} %bitcast.7) | data formatting | bytes 786432
  124.1 0.0 copy-done.1
  124.1 0.0 copy-start
  124.1 0.7 copy.12
  124.9 0.4 copy-done
  125.3 0.8 copy.13
Async XLA Ops:
  122.3 1.8 %copy-start.1 = (bf16[192,1024]{1,0:T(8,128)(2,1)S(1)}, bf16[192,1024]{1,0:T(8,128)(2,1)}, u32[]{:S(2)}) copy-start(bf16[192,1024]{1,0:T(8,128)(2,1)} %get-tuple-element.7) | copy-start | bytes 1179652
  124.1 1.2 copy-start
